TPU v7x, 256 devices: a whole 4x4x8 slice. The times are simulated.
256 devices in a mesh: outer: 64 (over y_lo, z, x), inner: 4 (over y_hi, core).
Axes of the slice: x: 4, y: 4 (y_hi: 2, y_lo: 2; y = y_hi * 2 + y_lo), z: 8, core: 2. Of those that a mesh axis runs over, the one named last changes fastest.
Arguments:
- queries: bfloat16 [32768, 4096], P(('outer', 'inner')), may hold values from -10 to 10
- keys: bfloat16 [32768, 512], P(('outer', 'inner')), may hold values from -10 to 10
- values: bfloat16 [32768, 512], P(('outer', 'inner')), may hold values from -6 to 6
- grad_out: bfloat16 [32768, 4096], P(('outer', 'inner')), may hold values from -6 to 6
- stretch_order: int32 [256, 2], replicated, may hold values from 0 to 511, as said below
- block_keep: int32 [256, 3, 2, 2], replicated, may hold values 0 or 1
Outputs:
- grad_queries: bfloat16 [32768, 4096], P(('outer', 'inner'))
- grad_keys: bfloat16 [32768, 512], P(('outer', 'inner'))
- grad_values: bfloat16 [32768, 512], P(('outer', 'inner'))
Inputs may be any that keep to these rules, and one draw needn't show every extreme that they name: `stretch_order`: each row holds two stretch numbers that add up to 511; over all rows every number of 0 to 511 appears once.
All inputs are finite; a program needn't handle non-finite values.
Results may differ from a plain program's by a relative error of at most 0.0084.
Values may be sent and summed in bfloat16 or wider, within the bound.
No kernel may reach another device: no remote copies, remote signals or barrier semaphores. Data moves between devices by JAX's collectives and lax.ppermute only.
A program may use at most 64 MiB of HBM per device.

v0:
```python
import jax
import jax.numpy as jnp
from jax import lax
from jax.sharding import PartitionSpec as P

HEAD_DIM = 128


neg_big = -1e30


def from_behind(block, axis, distance):
    devices = range(lax.axis_size(axis))
    route = [((i - distance) % len(devices), i) for i in devices]
    return lax.ppermute(block, axis, route)


def tile_mask(query_order, key_order, flags, row_count):
    line = jnp.arange(row_count, dtype=jnp.int32)
    query_pos = (query_order[:, None] * row_count + line[None, :]).reshape(-1)
    key_pos = (key_order[:, None] * row_count + line[None, :]).reshape(-1)
    flag_full = jnp.repeat(jnp.repeat(flags, row_count, axis=0), row_count, axis=1)
    return (flag_full > 0) & (key_pos[None, :] <= query_pos[:, None])


def masked_scores(query_rows, key_rows, mask):
    raw = jnp.einsum(
        "qkgd,jkd->kgqj", query_rows, key_rows, preferred_element_type=jnp.float32
    ) * HEAD_DIM ** (-0.5)
    return jnp.where(mask, raw, neg_big)


def stat_block(operands):
    query_rows, key_rows, mask = operands
    scores = masked_scores(query_rows, key_rows, mask)
    peak = jnp.max(scores, axis=-1)
    total = jnp.sum(jnp.where(mask, jnp.exp(scores - peak[..., None]), 0.0), axis=-1)
    return (peak, total)


def out_block(operands):
    query_rows, key_rows, value_rows, mask, log_norm = operands
    scores = masked_scores(query_rows, key_rows, mask)
    probs_low = jnp.where(mask, jnp.exp(scores - log_norm[..., None]), 0.0).astype(jnp.bfloat16)
    return jnp.einsum("kgqj,jkd->qkgd", probs_low, value_rows, preferred_element_type=jnp.float32)


def grad_block(operands):
    query_rows, grad_rows, log_norm, delta, key_rows, value_rows, mask = operands
    scores = masked_scores(query_rows, key_rows, mask)
    probs = jnp.where(mask, jnp.exp(scores - log_norm[..., None]), 0.0)
    probs_low = probs.astype(jnp.bfloat16)
    grad_probs = jnp.einsum(
        "qkgd,jkd->kgqj", grad_rows, value_rows, preferred_element_type=jnp.float32
    )
    grad_scores = (probs * (grad_probs - delta[..., None]) * HEAD_DIM ** (-0.5)).astype(
        jnp.bfloat16
    )
    grad_query = jnp.einsum(
        "kgqj,jkd->qkgd", grad_scores, key_rows, preferred_element_type=jnp.float32
    )
    grad_key = jnp.einsum(
        "kgqj,qkgd->jkd", grad_scores, query_rows, preferred_element_type=jnp.float32
    )
    grad_value = jnp.einsum(
        "kgqj,qkgd->jkd", probs_low, grad_rows, preferred_element_type=jnp.float32
    )
    return (grad_query, grad_key, grad_value)


def shards(queries, keys, values, grad_out, stretch_order, block_keep):
    row_count = keys.shape[0] // 2
    span = 2 * row_count
    kv_heads = keys.shape[1] // HEAD_DIM
    group = queries.shape[1] // (kv_heads * HEAD_DIM)
    width = kv_heads * HEAD_DIM
    n_inner = lax.axis_size("inner")
    n_outer = lax.axis_size("outer")
    pos_outer = lax.axis_index("outer")
    pos_inner = lax.axis_index("inner")
    holder = pos_outer * n_inner + pos_inner
    inner_prev = pos_outer * n_inner + (pos_inner + n_inner - 1) % n_inner
    outer_prev = (pos_outer + n_outer - 1) % n_outer * n_inner + pos_inner
    kv_in = from_behind((keys, values), "inner", 1)
    kv_out = from_behind((keys, values), "outer", 1)
    query_rows = queries.reshape(span, kv_heads, group, HEAD_DIM)
    grad_rows = grad_out.reshape(span, kv_heads, group, HEAD_DIM)
    own_order = lax.dynamic_index_in_dim(stretch_order, holder, 0, False)
    keep_row = lax.dynamic_index_in_dim(block_keep, holder, 0, False)
    forced = jnp.eye(2, dtype=jnp.int32)
    sources = [
        (keys, values, holder),
        (kv_in[0], kv_in[1], inner_prev),
        (kv_out[0], kv_out[1], outer_prev),
    ]
    tiles = []
    for source in range(3):
        src_keys, src_values, src_holder = sources[source]
        src_order = lax.dynamic_index_in_dim(stretch_order, src_holder, 0, False)
        flags = keep_row[source]
        if source == 0:
            flags = jnp.maximum(flags, forced)
        mask = tile_mask(own_order, src_order, flags, row_count)
        tiles.append(
            (
                src_keys.reshape(span, kv_heads, HEAD_DIM),
                src_values.reshape(span, kv_heads, HEAD_DIM),
                mask,
                jnp.any(mask),
            )
        )
    stats = [stat_block((query_rows, tile[0], tile[2])) for tile in tiles]
    peak = jnp.max(jnp.stack([entry[0] for entry in stats]), axis=0)
    total = jnp.zeros(peak.shape, jnp.float32)
    for entry in stats:
        total = total + entry[1] * jnp.exp(entry[0] - peak)
    log_norm = peak + jnp.log(total)
    outputs = jnp.zeros(query_rows.shape, jnp.float32)
    for tile in tiles:
        outputs = outputs + out_block((query_rows, tile[0], tile[1], tile[2], log_norm))
    delta = jnp.transpose(jnp.sum(grad_rows.astype(jnp.float32) * outputs, axis=-1), (1, 2, 0))
    query_grad = jnp.zeros(query_rows.shape, jnp.float32)
    key_grads = []
    value_grads = []
    for tile in tiles:
        pieces = grad_block((query_rows, grad_rows, log_norm, delta, tile[0], tile[1], tile[2]))
        query_grad = query_grad + pieces[0]
        key_grads.append(pieces[1].reshape(span, width))
        value_grads.append(pieces[2].reshape(span, width))
    grad_queries = query_grad.reshape(span, queries.shape[1]).astype(jnp.bfloat16)
    key_sum = key_grads[0]
    value_sum = value_grads[0]
    back_inner = from_behind((key_grads[1], value_grads[1]), "inner", -1)
    back_outer = from_behind((key_grads[2], value_grads[2]), "outer", -1)
    key_sum = key_sum + back_inner[0] + back_outer[0]
    value_sum = value_sum + back_inner[1] + back_outer[1]
    return (grad_queries, key_sum.astype(jnp.bfloat16), value_sum.astype(jnp.bfloat16))


def solution(mesh):
    in_specs = (
        P(("outer", "inner"), None),
        P(("outer", "inner"), None),
        P(("outer", "inner"), None),
        P(("outer", "inner"), None),
        P(),
        P(),
    )
    out_specs = (
        P(("outer", "inner"), None),
        P(("outer", "inner"), None),
        P(("outer", "inner"), None),
    )
    return jax.shard_map(shards, mesh=mesh, in_specs=in_specs, out_specs=out_specs, check_vma=False)
```

profile of v0, /device:TPU:1, one launch (start us, length us, event | category | flops | bytes accessed | tf_op | source)
XLA Modules:
  0.0 70.1 jit_solution(4677123932182790689)
XLA Ops:
  0.6 1.8 %copy.55 = bf16[128,512]{0,1:T(8,128)(2,1)} copy(bf16[128,512]{1,0:T(8,128)(2,1)} %param.7) | data formatting | bytes 262144 | tf_op args[1]
  2.5 2.0 %collective-permute-start.1 = (bf16[128,512]{0,1:T(8,128)(2,1)}, bf16[128,512]{0,1:T(8,128)(2,1)S(1)}, u32[]{:S(2)}, u32[]{:S(2)}) collective-permute-start(bf16[128,512]{0,1:T(8,128)(2,1)} %copy.55), channel_id=1, source_target_pairs={{252,0},{0,4},{4,8},{8,12},{12,16},{16,20},{20,24},{24,28},{28,32}... | collective-permute-start | bytes 393224 | tf_op jit(solution)/shard_map/ppermute | solution.py:15
  4.5 3.8 %collective-permute-start = (bf16[128,512]{0,1:T(8,128)(2,1)}, bf16[128,512]{0,1:T(8,128)(2,1)}, u32[]{:S(2)}, u32[]{:S(2)}) collective-permute-start(bf16[128,512]{0,1:T(8,128)(2,1)} %copy.55), channel_id=1, source_target_pairs={{3,0},{0,1},{1,2},{2,3},{7,4},{4,5},{5,6},{6,7},{11,8},{8,9},{9,10... | collective-permute-start | bytes 393224 | tf_op jit(solution)/shard_map/ppermute | solution.py:15
  8.3 1.2 %collective-permute-start.3 = (bf16[128,512]{1,0:T(8,128)(2,1)}, bf16[128,512]{1,0:T(8,128)(2,1)}, u32[]{:S(2)}, u32[]{:S(2)}) collective-permute-start(bf16[128,512]{1,0:T(8,128)(2,1)} %param.8), channel_id=1, source_target_pairs={{252,0},{0,4},{4,8},{8,12},{12,16},{16,20},{20,24},{24,28},{28,32}... | collective-permute-start | bytes 393224 | tf_op jit(solution)/shard_map/ppermute | solution.py:15
  9.8 0.9 %reshape.203 = bf16[128,4,128]{2,1,0:T(4,128)(2,1)S(1)} reshape(bf16[128,512]{1,0:T(8,128)(2,1)} %param.7) | data formatting | bytes 262144 | tf_op jit(solution)/shard_map/reshape | solution.py:106
  10.7 0.9 %reshape.207 = bf16[128,4,128]{2,1,0:T(4,128)(2,1)S(1)} reshape(bf16[128,512]{1,0:T(8,128)(2,1)} %param.8) | data formatting | bytes 262144 | tf_op jit(solution)/shard_map/reshape | solution.py:107
  11.6 1.0 %fusion.27 = (s32[2]{0:T(128)S(1)}, s32[2]{0:T(128)S(1)}, s32[2]{0:T(128)S(1)}) fusion(s32[256,2]{0,1:T(2,128)} %param.10, s32[]{:T(128)S(6)} %select_n.64, s32[]{:T(128)S(6)} %select_n.61, s32[]{:T(128)S(6)} %select_n.67), kind=kLoop, calls=%fused_computation.48 | loop fusion | flops 6 | bytes 60 | tf_op jit(solution)/shard_map/mul | solution.py:21
  17.7 1.3 %copy.62 = bf16[128,4096]{0,1:T(8,128)(2,1)} copy(bf16[128,4096]{1,0:T(8,128)(2,1)S(1)} %copy-done.14) | data formatting | bytes 2097152 | tf_op args[3]
  21.1 1.5 %fusion.39 = (f32[4,8,128]{2,1,0:T(8,128)S(1)}, f32[4,8,128,128]{2,3,1,0:T(8,128)S(1)}) fusion(bf16[128,4,128,1]{0,2,3,1:T(8,128)(2,1)} %bitcast.61, bf16[128,4,8,128]{0,3,2,1:T(8,128)(2,1)S(1)} %bitcast.158, pred[128,128]{0,1:T(8,128)(4,1)S(1)} %get-tuple-element.14), kind=kOutput, calls=%fused_computation.63 | convolution fusion | flops 135786496 | bytes 3309568 | tf_op jit(solution)/shard_map/qkgd,jkd->kgqj/dot_general | solution.py:27
  23.1 1.2 %fusion.20 = f32[4,128,128,1]{1,2,3,0:T(8,128)} fusion(bf16[128,4,8,128]{0,3,2,1:T(8,128)(2,1)S(1)} %bitcast.163, f32[4,8,128,128]{2,3,1,0:T(8,128)S(1)} %get-tuple-element.22, f32[4,8,128]{2,1,0:T(8,128)S(1)} %log_add_fusion, pred[128,128]{0,1:T(8,128)(4,1)S(1)} %get-tuple-element.16), kind=kOutput, calls=%fused_computation.32 | convolution fusion | flops 135790592 | bytes 3440640 | tf_op jit(solution)/shard_map/kgqj,qkgd->jkd/dot_general | solution.py:65
  24.3 1.2 %fusion.16 = f32[4,128,128,1]{1,2,3,0:T(8,128)} fusion(bf16[128,4,8,128]{0,3,2,1:T(8,128)(2,1)S(1)} %bitcast.164, f32[4,8,128,128]{2,3,1,0:T(8,128)S(1)} %get-tuple-element.20, f32[4,8,128]{2,1,0:T(8,128)S(1)} %log_add_fusion, pred[128,128]{0,1:T(8,128)(4,1)S(1)} %get-tuple-element.14), kind=kOutput, calls=%fused_computation.30 | convolution fusion | flops 135790592 | bytes 3440640 | tf_op jit(solution)/shard_map/kgqj,qkgd->jkd/dot_general | solution.py:65
  25.5 1.0 %copy.67 = bf16[128,512]{0,1:T(8,128)(2,1)S(1)} copy(bf16[128,512]{1,0:T(8,128)(2,1)} %collective-permute-done.2) | data formatting | bytes 262144 | tf_op jit(solution)/shard_map/ppermute | solution.py:15
  26.5 3.5 %fusion.18 = f32[4,8,128,128]{2,3,1,0:T(8,128)} fusion(bf16[128,4,128,1]{0,2,3,1:T(8,128)(2,1)S(1)} %bitcast.172, f32[4,8,128,128]{2,3,1,0:T(8,128)} %copy-done.3, f32[4,8,128]{2,1,0:T(8,128)S(1)} %log_add_fusion, pred[128,128]{0,1:T(8,128)(4,1)} %copy-done.23), kind=kOutput, calls=%fused_computation.31 | convolution fusion | flops 135790592 | bytes 4358144 | tf_op jit(solution)/shard_map/kgqj,jkd->qkgd/dot_general | solution.py:45
  30.1 1.8 %fusion.22 = f32[4,8,128,128]{2,3,1,0:T(8,128)} fusion(bf16[128,4,128,1]{0,2,3,1:T(8,128)(2,1)S(1)} %copy.101, f32[4,8,128,128]{2,3,1,0:T(8,128)S(1)} %copy-done.1, f32[4,8,128]{2,1,0:T(8,128)S(1)} %log_add_fusion, pred[128,128]{0,1:T(8,128)(4,1)S(1)} %copy-done.18), kind=kOutput, calls=%fused_computation.33 | convolution fusion | flops 135790592 | bytes 4358144 | tf_op jit(solution)/shard_map/kgqj,jkd->qkgd/dot_general | solution.py:45
  31.9 1.2 %fusion.13 = f32[4,128,128,1]{1,2,3,0:T(8,128)} fusion(bf16[128,4,8,128]{0,3,2,1:T(8,128)(2,1)S(1)} %bitcast.165, f32[4,8,128,128]{2,3,1,0:T(8,128)S(1)} %get-tuple-element.18, f32[4,8,128]{2,1,0:T(8,128)S(1)} %log_add_fusion, pred[128,128]{0,1:T(8,128)(4,1)S(1)} %copy-done.21), kind=kOutput, calls=%fused_computation.29 | convolution fusion | flops 135790592 | bytes 3440640 | tf_op jit(solution)/shard_map/kgqj,qkgd->jkd/dot_general | solution.py:65
  33.1 1.0 %copy.69 = bf16[128,512]{0,1:T(8,128)(2,1)S(1)} copy(bf16[128,512]{1,0:T(8,128)(2,1)} %collective-permute-done.3) | data formatting | bytes 262144 | tf_op jit(solution)/shard_map/ppermute | solution.py:15
  34.2 3.4 %fusion.6 = f32[128,4,8]{0,2,1:T(8,128)S(1)} fusion(f32[4,8,128,128]{2,3,1,0:T(8,128)} %fusion.22, f32[4,8,128,128]{2,3,1,0:T(8,128)} %fusion.18, bf16[128,4,8,128]{0,3,2,1:T(8,128)(2,1)} %bitcast.162, bf16[128,4,128,1]{0,2,3,1:T(8,128)(2,1)S(1)} %bitcast.170, f32[4,8,128,128]{2,3,1,0:T(8,128)S(1)} %get-tuple-element.18, f32[4,8,128]{2,1,0:T(8,128)S(1)} %log_add_fusion, ...), kind=kOutput, calls=%fused_computation.9 | convolution fusion | flops 138407936 | bytes 7520256 | tf_op jit(solution)/shard_map/kgqj,jkd->qkgd/dot_general | solution.py:45
  38.4 1.7 %fusion.2 = bf16[4,8,128,128]{2,3,1,0:T(8,128)(2,1)} fusion(f32[4,8,128,128]{2,3,1,0:T(8,128)S(1)} %get-tuple-element.18, bf16[128,4,128,1]{0,2,3,1:T(8,128)(2,1)S(1)} %bitcast.171, bf16[128,4,8,128]{0,3,2,1:T(8,128)(2,1)S(1)} %bitcast.167, f32[4,8,128]{2,1,0:T(8,128)S(1)} %bitcast.182, f32[4,8,128]{2,1,0:T(8,128)S(1)} %log_add_fusion, ...), kind=kOutput, calls=%fused_computation.3 | convolution fusion | flops 137363456 | bytes 4374528 | tf_op jit(solution)/shard_map/qkgd,jkd->kgqj/dot_general | solution.py:53
  41.0 1.1 %fusion.42 = f32[4,128,128,1]{1,2,3,0:T(8,128)} fusion(bf16[4,8,128,128]{2,3,1,0:T(8,128)(2,1)S(1)} %fusion.5, bf16[128,4,8,128]{0,3,2,1:T(8,128)(2,1)S(1)} %bitcast.159), kind=kOutput, calls=%fused_computation.66 | convolution fusion | flops 134217728 | bytes 2359296 | tf_op jit(solution)/shard_map/kgqj,qkgd->jkd/dot_general | solution.py:62
  42.1 2.8 %fusion.45 = f32[4,8,128,128]{2,3,1,0:T(8,128)} fusion(bf16[128,4,128,1]{0,2,3,1:T(8,128)(2,1)} %bitcast.61, bf16[4,8,128,128]{2,3,1,0:T(8,128)(2,1)S(1)} %fusion.5), kind=kOutput, calls=%fused_computation.69 | convolution fusion | flops 134217728 | bytes 3276800 | tf_op jit(solution)/shard_map/kgqj,jkd->qkgd/dot_general | solution.py:59
  44.9 1.8 %copy.90 = f32[128,512]{1,0:T(8,128)} copy(f32[128,512]{0,1:T(8,128)} %bitcast.185) | data formatting | bytes 524288 | tf_op jit(solution)/shard_map/reshape | solution.py:129
  46.6 1.8 %copy.93 = f32[128,512]{1,0:T(8,128)} copy(f32[128,512]{0,1:T(8,128)} %bitcast.186) | data formatting | bytes 524288 | tf_op jit(solution)/shard_map/reshape | solution.py:129
  48.4 5.2 %collective-permute-start.7 = (f32[128,512]{1,0:T(8,128)}, f32[128,512]{1,0:T(8,128)}, u32[]{:S(2)}, u32[]{:S(2)}) collective-permute-start(f32[128,512]{1,0:T(8,128)} %copy.93), channel_id=1, source_target_pairs={{4,0},{8,4},{12,8},{16,12},{20,16},{24,20},{28,24},{32,28},{36,32}... | collective-permute-start | bytes 786440 | tf_op jit(solution)/shard_map/ppermute | solution.py:15
  54.2 1.1 %fusion.43 = f32[4,128,128,1]{1,2,3,0:T(8,128)} fusion(bf16[4,8,128,128]{2,3,1,0:T(8,128)(2,1)S(1)} %copy-done.8, bf16[128,4,8,128]{0,3,2,1:T(8,128)(2,1)S(1)} %bitcast.160), kind=kOutput, calls=%fused_computation.67 | convolution fusion | flops 134217728 | bytes 2359296 | tf_op jit(solution)/shard_map/kgqj,qkgd->jkd/dot_general | solution.py:62
  55.3 1.8 %copy.83 = f32[128,512]{1,0:T(8,128)} copy(f32[128,512]{0,1:T(8,128)} %bitcast.174) | data formatting | bytes 524288 | tf_op jit(solution)/shard_map/reshape | solution.py:128
  57.1 1.8 %copy.87 = f32[128,512]{1,0:T(8,128)} copy(f32[128,512]{0,1:T(8,128)} %bitcast.176) | data formatting | bytes 524288 | tf_op jit(solution)/shard_map/reshape | solution.py:128
  58.9 1.7 %collective-permute-start.5 = (f32[128,512]{1,0:T(8,128)}, f32[128,512]{1,0:T(8,128)}, u32[]{:S(2)}, u32[]{:S(2)}) collective-permute-start(f32[128,512]{1,0:T(8,128)} %copy.87), channel_id=1, source_target_pairs={{4,0},{8,4},{12,8},{16,12},{20,16},{24,20},{28,24},{32,28},{36,32}... | collective-permute-start | bytes 786440 | tf_op jit(solution)/shard_map/ppermute | solution.py:15
  62.0 1.5 %add_convert_fusion = bf16[4,8,128,128]{2,3,1,0:T(8,128)(2,1)} fusion(f32[4,8,128,128]{2,3,1,0:T(8,128)S(1)} %fusion.44, f32[4,8,128,128]{2,3,1,0:T(8,128)S(1)} %copy-done.9, bf16[128,4,128,1]{0,2,3,1:T(8,128)(2,1)S(1)} %bitcast.178, bf16[4,8,128,128]{2,3,1,0:T(8,128)(2,1)S(1)} %copy-done.8), kind=kOutput, calls=%fused_computation.17 | convolution fusion | flops 135790592 | bytes 6422528 | tf_op jit(solution)/shard_map/kgqj,jkd->qkgd/dot_general | solution.py:59
  63.9 1.1 %copy.91 = f32[128,512]{1,0:T(8,128)S(1)} copy(f32[128,512]{0,1:T(8,128)} %bitcast.184) | data formatting | bytes 524288 | tf_op jit(solution)/shard_map/reshape | solution.py:129
  65.1 1.3 %copy.94 = bf16[128,4096]{1,0:T(8,128)(2,1)} copy(bf16[128,4096]{0,1:T(8,128)(2,1)S(1)} %bitcast.169) | data formatting | bytes 2097152
  66.4 1.7 %add_convert_fusion.1 = bf16[128,512]{1,0:T(8,128)(2,1)} fusion(f32[128,512]{1,0:T(8,128)} %collective-permute-done.7, f32[128,512]{1,0:T(8,128)S(1)} %copy.91, f32[128,512]{1,0:T(8,128)} %collective-permute-done.6), kind=kLoop, calls=%fused_computation.27 | loop fusion | flops 196608 | bytes 917504 | tf_op jit(solution)/shard_map/convert_element_type | solution.py:137
  68.4 1.7 %add_convert_fusion.2 = bf16[128,512]{1,0:T(8,128)(2,1)} fusion(f32[128,512]{1,0:T(8,128)} %collective-permute-done.5, f32[128,512]{1,0:T(8,128)S(1)} %copy.84, f32[128,512]{1,0:T(8,128)} %collective-permute-done.4), kind=kLoop, calls=%fused_computation.28 | loop fusion | flops 196608 | bytes 917504 | tf_op jit(solution)/shard_map/convert_element_type | solution.py:137
  (97 shorter events, 12.0 us)
Async XLA Ops:
  0.6 16.3 %copy-start.13 = (bf16[128,4096]{1,0:T(8,128)(2,1)S(1)}, bf16[128,4096]{1,0:T(8,128)(2,1)}, u32[]{:S(2)}) copy-start(bf16[128,4096]{1,0:T(8,128)(2,1)} %param.6) | copy-start | bytes 3145732
  0.6 17.0 %copy-start.14 = (bf16[128,4096]{1,0:T(8,128)(2,1)S(1)}, bf16[128,4096]{1,0:T(8,128)(2,1)}, u32[]{:S(2)}) copy-start(bf16[128,4096]{1,0:T(8,128)(2,1)} %param.9) | copy-start | bytes 3145732
  2.5 17.6 %collective-permute-start.1 = (bf16[128,512]{0,1:T(8,128)(2,1)}, bf16[128,512]{0,1:T(8,128)(2,1)S(1)}, u32[]{:S(2)}, u32[]{:S(2)}) collective-permute-start(bf16[128,512]{0,1:T(8,128)(2,1)} %copy.55), channel_id=1, source_target_pairs={{252,0},{0,4},{4,8},{8,12},{12,16},{16,20},{20,24},{24,28},{28,32}... | collective-permute-start | bytes 393224 | tf_op jit(solution)/shard_map/ppermute | solution.py:15
  4.5 16.6 %collective-permute-start = (bf16[128,512]{0,1:T(8,128)(2,1)}, bf16[128,512]{0,1:T(8,128)(2,1)}, u32[]{:S(2)}, u32[]{:S(2)}) collective-permute-start(bf16[128,512]{0,1:T(8,128)(2,1)} %copy.55), channel_id=1, source_target_pairs={{3,0},{0,1},{1,2},{2,3},{7,4},{4,5},{5,6},{6,7},{11,8},{8,9},{9,10... | collective-permute-start | bytes 393224 | tf_op jit(solution)/shard_map/ppermute | solution.py:15
  8.3 24.8 %collective-permute-start.3 = (bf16[128,512]{1,0:T(8,128)(2,1)}, bf16[128,512]{1,0:T(8,128)(2,1)}, u32[]{:S(2)}, u32[]{:S(2)}) collective-permute-start(bf16[128,512]{1,0:T(8,128)(2,1)} %param.8), channel_id=1, source_target_pairs={{252,0},{0,4},{4,8},{8,12},{12,16},{16,20},{20,24},{24,28},{28,32}... | collective-permute-start | bytes 393224 | tf_op jit(solution)/shard_map/ppermute | solution.py:15
  9.5 16.0 %collective-permute-start.2 = (bf16[128,512]{1,0:T(8,128)(2,1)}, bf16[128,512]{1,0:T(8,128)(2,1)}, u32[]{:S(2)}, u32[]{:S(2)}) collective-permute-start(bf16[128,512]{1,0:T(8,128)(2,1)} %param.8), channel_id=1, source_target_pairs={{3,0},{0,1},{1,2},{2,3},{7,4},{4,5},{5,6},{6,7},{11,8},{8,9},{9,10... | collective-permute-start | bytes 393224 | tf_op jit(solution)/shard_map/ppermute | solution.py:15
  17.7 1.3 %copy-start.25 = (s32[128]{0:T(128)S(1)}, s32[128]{0:T(128)}, u32[]{:S(2)}) copy-start(s32[128]{0:T(128)} %add.192) | copy-start | bytes 1540
  19.1 1.5 %copy-start.20 = (pred[128,128]{0,1:T(8,128)(4,1)}, pred[128,128]{0,1:T(8,128)(4,1)S(1)}, u32[]{:S(2)}) copy-start(pred[128,128]{0,1:T(8,128)(4,1)S(1)} %get-tuple-element.15) | copy-start | bytes 49156
  19.1 3.9 %copy-start.17 = (pred[128,128]{0,1:T(8,128)(4,1)}, pred[128,128]{0,1:T(8,128)(4,1)S(1)}, u32[]{:S(2)}) copy-start(pred[128,128]{0,1:T(8,128)(4,1)S(1)} %get-tuple-element.16) | copy-start | bytes 49156
  19.1 5.2 %copy-start.23 = (pred[128,128]{0,1:T(8,128)(4,1)}, pred[128,128]{0,1:T(8,128)(4,1)S(1)}, u32[]{:S(2)}) copy-start(pred[128,128]{0,1:T(8,128)(4,1)S(1)} %get-tuple-element.14) | copy-start | bytes 49156
  19.7 3.4 %copy-start = (f32[4,8,128,128]{2,3,1,0:T(8,128)}, f32[4,8,128,128]{2,3,1,0:T(8,128)S(1)}, u32[]{:S(2)}) copy-start(f32[4,8,128,128]{2,3,1,0:T(8,128)S(1)} %get-tuple-element.22) | copy-start | bytes 6291460
  21.1 2.0 %copy-start.5 = (bf16[128,4096]{0,1:T(8,128)(2,1)S(1)}, bf16[128,4096]{0,1:T(8,128)(2,1)}, u32[]{:S(2)}) copy-start(bf16[128,4096]{0,1:T(8,128)(2,1)} %copy.62) | copy-start | bytes 3145732
  22.6 1.7 %copy-start.3 = (f32[4,8,128,128]{2,3,1,0:T(8,128)}, f32[4,8,128,128]{2,3,1,0:T(8,128)S(1)}, u32[]{:S(2)}) copy-start(f32[4,8,128,128]{2,3,1,0:T(8,128)S(1)} %get-tuple-element.20) | copy-start | bytes 6291460
  26.5 3.6 %copy-start.11 = (bf16[128,512]{0,1:T(8,128)(2,1)}, bf16[128,512]{0,1:T(8,128)(2,1)S(1)}, u32[]{:S(2)}) copy-start(bf16[128,512]{0,1:T(8,128)(2,1)S(1)} %copy.67) | copy-start | bytes 393220
  26.5 3.6 %copy-start.1 = (f32[4,8,128,128]{2,3,1,0:T(8,128)S(1)}, f32[4,8,128,128]{2,3,1,0:T(8,128)}, u32[]{:S(2)}) copy-start(f32[4,8,128,128]{2,3,1,0:T(8,128)} %copy-done) | copy-start | bytes 6291460
  26.5 3.6 %copy-start.18 = (pred[128,128]{0,1:T(8,128)(4,1)S(1)}, pred[128,128]{0,1:T(8,128)(4,1)}, u32[]{:S(2)}) copy-start(pred[128,128]{0,1:T(8,128)(4,1)} %copy-done.17) | copy-start | bytes 49156
  30.1 1.8 %copy-start.6 = (bf16[128,4096]{0,1:T(8,128)(2,1)S(1)}, bf16[128,4096]{0,1:T(8,128)(2,1)}, u32[]{:S(2)}) copy-start(bf16[128,4096]{0,1:T(8,128)(2,1)} %copy.62) | copy-start | bytes 3145732
  30.1 1.8 %copy-start.21 = (pred[128,128]{0,1:T(8,128)(4,1)S(1)}, pred[128,128]{0,1:T(8,128)(4,1)}, u32[]{:S(2)}) copy-start(pred[128,128]{0,1:T(8,128)(4,1)} %copy-done.20) | copy-start | bytes 49156
  34.1 3.4 %copy-start.4 = (f32[4,8,128,128]{2,3,1,0:T(8,128)S(1)}, f32[4,8,128,128]{2,3,1,0:T(8,128)}, u32[]{:S(2)}) copy-start(f32[4,8,128,128]{2,3,1,0:T(8,128)} %copy-done.3) | copy-start | bytes 6291460
  34.1 3.4 %copy-start.7 = (bf16[128,4096]{0,1:T(8,128)(2,1)S(1)}, bf16[128,4096]{0,1:T(8,128)(2,1)}, u32[]{:S(2)}) copy-start(bf16[128,4096]{0,1:T(8,128)(2,1)} %copy.62) | copy-start | bytes 3145732
  34.1 3.4 %copy-start.12 = (bf16[128,512]{0,1:T(8,128)(2,1)S(1)}, bf16[128,512]{0,1:T(8,128)(2,1)}, u32[]{:S(2)}) copy-start(bf16[128,512]{0,1:T(8,128)(2,1)} %copy-done.11) | copy-start | bytes 393220
  34.2 3.4 %copy-start.24 = (pred[128,128]{0,1:T(8,128)(4,1)S(1)}, pred[128,128]{0,1:T(8,128)(4,1)}, u32[]{:S(2)}) copy-start(pred[128,128]{0,1:T(8,128)(4,1)} %copy-done.23) | copy-start | bytes 49156
  38.4 1.8 %copy-start.2 = (f32[4,8,128,128]{2,3,1,0:T(8,128)S(1)}, f32[4,8,128,128]{2,3,1,0:T(8,128)}, u32[]{:S(2)}) copy-start(f32[4,8,128,128]{2,3,1,0:T(8,128)} %copy-done) | copy-start | bytes 6291460
  38.4 1.7 %copy-start.19 = (pred[128,128]{0,1:T(8,128)(4,1)S(1)}, pred[128,128]{0,1:T(8,128)(4,1)}, u32[]{:S(2)}) copy-start(pred[128,128]{0,1:T(8,128)(4,1)} %copy-done.17) | copy-start | bytes 49156
  42.1 12.1 %copy-start.8 = (bf16[4,8,128,128]{2,3,1,0:T(8,128)(2,1)S(1)}, bf16[4,8,128,128]{2,3,1,0:T(8,128)(2,1)}, u32[]{:S(2)}) copy-start(bf16[4,8,128,128]{2,3,1,0:T(8,128)(2,1)} %fusion.2) | copy-start | bytes 3145732
  48.4 18.0 %collective-permute-start.7 = (f32[128,512]{1,0:T(8,128)}, f32[128,512]{1,0:T(8,128)}, u32[]{:S(2)}, u32[]{:S(2)}) collective-permute-start(f32[128,512]{1,0:T(8,128)} %copy.93), channel_id=1, source_target_pairs={{4,0},{8,4},{12,8},{16,12},{20,16},{24,20},{28,24},{32,28},{36,32}... | collective-permute-start | bytes 786440 | tf_op jit(solution)/shard_map/ppermute | solution.py:15
  53.6 12.8 %collective-permute-start.6 = (f32[128,512]{1,0:T(8,128)}, f32[128,512]{1,0:T(8,128)}, u32[]{:S(2)}, u32[]{:S(2)}) collective-permute-start(f32[128,512]{1,0:T(8,128)} %copy.90), channel_id=1, source_target_pairs={{1,0},{2,1},{3,2},{0,3},{5,4},{6,5},{7,6},{4,7},{9,8},{10,9},{11,1... | collective-permute-start | bytes 786440 | tf_op jit(solution)/shard_map/ppermute | solution.py:15
  55.3 6.7 %copy-start.16 = (bf16[128,512]{0,1:T(8,128)(2,1)S(1)}, bf16[128,512]{0,1:T(8,128)(2,1)}, u32[]{:S(2)}) copy-start(bf16[128,512]{0,1:T(8,128)(2,1)} %copy-done.15) | copy-start | bytes 393220
  58.9 3.1 %copy-start.9 = (f32[4,8,128,128]{2,3,1,0:T(8,128)S(1)}, f32[4,8,128,128]{2,3,1,0:T(8,128)}, u32[]{:S(2)}) copy-start(f32[4,8,128,128]{2,3,1,0:T(8,128)} %fusion.45) | copy-start | bytes 6291460
  58.9 9.3 %collective-permute-start.5 = (f32[128,512]{1,0:T(8,128)}, f32[128,512]{1,0:T(8,128)}, u32[]{:S(2)}, u32[]{:S(2)}) collective-permute-start(f32[128,512]{1,0:T(8,128)} %copy.87), channel_id=1, source_target_pairs={{4,0},{8,4},{12,8},{16,12},{20,16},{24,20},{28,24},{32,28},{36,32}... | collective-permute-start | bytes 786440 | tf_op jit(solution)/shard_map/ppermute | solution.py:15
  60.7 7.8 %collective-permute-start.4 = (f32[128,512]{1,0:T(8,128)}, f32[128,512]{1,0:T(8,128)}, u32[]{:S(2)}, u32[]{:S(2)}) collective-permute-start(f32[128,512]{1,0:T(8,128)} %copy.83), channel_id=1, source_target_pairs={{1,0},{2,1},{3,2},{0,3},{5,4},{6,5},{7,6},{4,7},{9,8},{10,9},{11,1... | collective-permute-start | bytes 786440 | tf_op jit(solution)/shard_map/ppermute | solution.py:15
  63.4 1.7 %copy-start.10 = (bf16[4,8,128,128]{2,3,1,0:T(8,128)(2,1)S(1)}, bf16[4,8,128,128]{2,3,1,0:T(8,128)(2,1)}, u32[]{:S(2)}) copy-start(bf16[4,8,128,128]{2,3,1,0:T(8,128)(2,1)} %add_convert_fusion) | copy-start | bytes 3145732
  (3 other events, 3.1 us)
where the time goes:
time: 70.6 us; the launch traced here: 70.1 us
  matrix products  25.4 us (36%)
  local copies, waits for them, and re-layouts  20.9 us (30%)
  starting transfers between devices  15.6 us (22%)
  other arithmetic  6.78 us (10%)
  between operations  1.13 us (2%)
    ppermute x8, starting transfers between devices, from_behind(): return lax.ppermute(block, axis, route)  15.6 us
    dot_general x3, matrix products, out_block(): jnp.einsum('kgqj,jkd->qkgd', probs_low, value_rows, preferred_element_typ...  8.71 us
    reshape x3, local copies, waits for them, and re-layouts, shards(): value_grads.append(pieces[2].reshape(span, width))  4.66 us
    dot_general x3, matrix products, grad_block(): jnp.einsum('kgqj,jkd->qkgd', grad_scores, key_rows, preferred_element_typ...  4.63 us
    unnamed x57, local copies, waits for them, and re-layouts  4.56 us
    reshape x3, local copies, waits for them, and re-layouts, shards(): key_grads.append(pieces[1].reshape(span, width))  3.73 us
    dot_general x3, matrix products, grad_block(): jnp.einsum('kgqj,qkgd->jkd', probs_low, grad_rows, preferred_element_type...  3.56 us
    dot_general x3, matrix products, grad_block(): jnp.einsum('qkgd,jkd->kgqj', grad_rows, value_rows, preferred_element_typ...  3.29 us
  transfers between devices with their start and end apart: 8, of which 1 were waited for; matrix products, arithmetic and copies ran while one was open for 49% of the time, Pallas kernels for 0%

commit v1 on v0

v1 whole, which is shorter than its diff:
```python
import functools

import jax
import jax.numpy as jnp
from jax import lax
from jax.experimental import pallas as pl
from jax.experimental.pallas import tpu as pltpu
from jax.sharding import PartitionSpec as P

HEAD_DIM = 128
SCALE = HEAD_DIM ** -0.5
LOG2E = 1.4426950408889634
NEG_BIG = -1e30
VMEM = 16 * 1024 * 1024
NT = (((1,), (1,)), ((), ()))
NN = (((1,), (0,)), ((), ()))
TN = (((0,), (0,)), ((), ()))


def dot(a, b, dims):
    return lax.dot_general(a, b, dims, preferred_element_type=jnp.float32)


def from_behind(block, axis, distance):
    size = lax.axis_size(axis)
    return lax.ppermute(block, axis, [((i - distance) % size, i) for i in range(size)])


def head(ref, h, count=1):
    return ref[:, h * HEAD_DIM : (h + count) * HEAD_DIM]


def stack_heads(ref, first, count):
    return jnp.concatenate([head(ref, first + e) for e in range(count)], axis=0)


def stack_sources(refs, h):
    return jnp.concatenate([head(ref, h) for ref in refs], axis=0)


def fill_bias(meta, bias, stretch):
    lane = lax.broadcasted_iota(jnp.int32, (stretch, 2 * stretch), 1)
    line = lax.broadcasted_iota(jnp.int32, (stretch, 2 * stretch), 0)
    first = lane < stretch
    query_pos = jnp.where(first, meta[0] * stretch + lane, (meta[1] - 1) * stretch + lane)
    for s in range(3):
        for b in range(2):
            flags = [meta[6 + s * 4 + a * 2 + b] for a in range(2)]
            if s == 0:
                flags[b] = jnp.int32(1)
            flag = jnp.where(first, flags[0], flags[1])
            key_pos = meta[2 * s + b] * stretch + line
            allowed = (flag > 0) & (key_pos <= query_pos)
            row = (2 * s + b) * stretch
            bias[row : row + stretch, :] = jnp.where(allowed, 0.0, NEG_BIG)


def stage_kernel(meta, queries, grads, q, g, bias, sems):
    copies = [
        pltpu.make_async_copy(queries, q, sems.at[0]),
        pltpu.make_async_copy(grads, g, sems.at[1]),
    ]
    for copy in copies:
        copy.start()
    fill_bias(meta, bias, bias.shape[1] // 2)
    for copy in copies:
        copy.wait()


def probs_kernel(group, bias, q, g, ks, ki, ko, probs, dvs, dvi, dvo):
    span = q.shape[0]
    for h in range(ks.shape[1] // HEAD_DIM):
        lanes = slice(h * HEAD_DIM, (h + 1) * HEAD_DIM)
        keys = stack_sources((ks, ki, ko), h)
        for pair in range(group // 2):
            cols = slice(2 * pair * HEAD_DIM, (2 * pair + 2) * HEAD_DIM)
            query = stack_heads(q, h * group + 2 * pair, 2)
            wide = jnp.concatenate([bias[...], bias[...]], axis=1)
            scores = dot(keys, query, NT) * (SCALE * LOG2E) + wide
            peak = jnp.max(scores, axis=0, keepdims=True)
            raised = jnp.exp2(scores - peak)
            total = jnp.sum(raised, axis=0, keepdims=True)
            probs[h, :, cols] = (raised * (1.0 / total)).astype(jnp.bfloat16)
        out = dot(probs[h], stack_heads(g, h * group, group), NN)
        dvs[:, lanes] = out[:span]
        dvi[:, lanes] = out[span : 2 * span].astype(jnp.bfloat16)
        dvo[:, lanes] = out[2 * span :].astype(jnp.bfloat16)


def scores_kernel(group, q, g, vs, vi, vo, probs, dscores, dks, dki, dko):
    span = q.shape[0]
    for h in range(vs.shape[1] // HEAD_DIM):
        lanes = slice(h * HEAD_DIM, (h + 1) * HEAD_DIM)
        values = stack_sources((vs, vi, vo), h)
        for pair in range(group // 2):
            cols = slice(2 * pair * HEAD_DIM, (2 * pair + 2) * HEAD_DIM)
            grad_probs = dot(values, stack_heads(g, h * group + 2 * pair, 2), NT)
            weight = probs[h, :, cols].astype(jnp.float32)
            delta = jnp.sum(weight * grad_probs, axis=0, keepdims=True)
            dscores[h, :, cols] = (weight * ((grad_probs - delta) * SCALE)).astype(jnp.bfloat16)
        out = dot(dscores[h], stack_heads(q, h * group, group), NN)
        dks[:, lanes] = out[:span]
        dki[:, lanes] = out[span : 2 * span].astype(jnp.bfloat16)
        dko[:, lanes] = out[2 * span :].astype(jnp.bfloat16)


def queries_kernel(group, ks, ki, ko, dscores, dq):
    for h in range(ks.shape[1] // HEAD_DIM):
        keys = stack_sources((ks, ki, ko), h)
        for g in range(group):
            lanes = slice((h * group + g) * HEAD_DIM, (h * group + g + 1) * HEAD_DIM)
            cols = slice(g * HEAD_DIM, (g + 1) * HEAD_DIM)
            dq[:, lanes] = dot(dscores[h, :, cols], keys, TN).astype(jnp.bfloat16)


def add_kernel(a, b, c, d, e, f, dk, dv):
    dk[...] = (a[...] + b[...].astype(jnp.float32) + c[...].astype(jnp.float32)).astype(dk.dtype)
    dv[...] = (d[...] + e[...].astype(jnp.float32) + f[...].astype(jnp.float32)).astype(dv.dtype)


def shards(queries, keys, values, grad_out, stretch_order, block_keep):
    span = keys.shape[0]
    width = keys.shape[1]
    kv_heads = width // HEAD_DIM
    group = queries.shape[1] // width
    n_inner = lax.axis_size("inner")
    n_outer = lax.axis_size("outer")
    pos_outer = lax.axis_index("outer")
    pos_inner = lax.axis_index("inner")
    holder = pos_outer * n_inner + pos_inner
    inner_prev = pos_outer * n_inner + (pos_inner + n_inner - 1) % n_inner
    outer_prev = (pos_outer + n_outer - 1) % n_outer * n_inner + pos_inner
    k_out = from_behind(keys, "outer", 1)
    k_in = from_behind(keys, "inner", 1)
    v_out = from_behind(values, "outer", 1)
    v_in = from_behind(values, "inner", 1)
    orders = [lax.dynamic_index_in_dim(stretch_order, h, 0, False) for h in (holder, inner_prev, outer_prev)]
    keep = lax.dynamic_index_in_dim(block_keep, holder, 0, False).reshape(-1)
    meta = jnp.concatenate(orders + [keep])

    f32, bf16 = jnp.float32, jnp.bfloat16
    vmem = pl.BlockSpec(memory_space=pltpu.VMEM)
    smem = pl.BlockSpec(memory_space=pltpu.SMEM)
    hbm = pl.BlockSpec(memory_space=pl.ANY)
    rows = jax.ShapeDtypeStruct(queries.shape, bf16)
    table = jax.ShapeDtypeStruct((kv_heads, 3 * span, group * HEAD_DIM), bf16)
    kv32 = jax.ShapeDtypeStruct((span, width), f32)
    kv16 = jax.ShapeDtypeStruct((span, width), bf16)
    flops = 2 * span * queries.shape[1] * 3 * span

    def call(kernel, ins, out_shape, ops, scratch=()):
        return pl.pallas_call(
            kernel,
            in_specs=ins,
            out_specs=[vmem] * len(out_shape),
            out_shape=out_shape,
            scratch_shapes=scratch,
            compiler_params=pltpu.CompilerParams(vmem_limit_bytes=VMEM),
            cost_estimate=pl.CostEstimate(flops=ops * flops, bytes_accessed=2**20, transcendentals=0),
        )

    q, g, bias = call(
        stage_kernel,
        [smem, hbm, hbm],
        [rows, rows, jax.ShapeDtypeStruct((3 * span, span), f32)],
        1,
        [pltpu.SemaphoreType.DMA((2,))],
    )(meta, queries, grad_out)
    probs, dvs, dvi, dvo = call(
        functools.partial(probs_kernel, group), [vmem] * 6, [table, kv32, kv16, kv16], 2
    )(bias, q, g, keys, k_in, k_out)
    dv_out = from_behind(dvo, "outer", -1)
    dv_in = from_behind(dvi, "inner", -1)
    dscores, dks, dki, dko = call(
        functools.partial(scores_kernel, group), [vmem] * 6, [table, kv32, kv16, kv16], 2
    )(q, g, values, v_in, v_out, probs)
    dk_out = from_behind(dko, "outer", -1)
    dk_in = from_behind(dki, "inner", -1)
    (dq,) = call(functools.partial(queries_kernel, group), [vmem] * 4, [rows], 1)(keys, k_in, k_out, dscores)
    dk, dv = call(add_kernel, [vmem] * 6, [kv16, kv16], 0)(dks, dk_in, dk_out, dvs, dv_in, dv_out)
    return dq, dk, dv


def solution(mesh):
    rows = P(("outer", "inner"), None)
    return jax.shard_map(
        shards, mesh=mesh, in_specs=(rows, rows, rows, rows, P(), P()), out_specs=(rows, rows, rows), check_vma=False
    )
```

time: 70.6 us -> 36.2 us (0.51)
  matrix products: 25.4 us -> 0 us
  local copies, waits for them, and re-layouts: 20.9 us -> 4.7 us
  Pallas kernels: 0 us -> 9.95 us
  waiting for transfers between devices: 0.26 us -> 7.97 us
  other arithmetic: 6.78 us -> 0.08 us
  starting transfers between devices: 15.6 us -> 12.5 us
    dot_general x18 -> x0, matrix products: 25.4 us -> none  [the longest x3 8.71 us: out_block(): jnp.einsum('kgqj,jkd->qkgd', probs_low, value_rows, preferred_element_typ...]
    reshape x11 -> x1, local copies, waits for them, and re-layouts: 11.2 us -> 0.09 us  [shards(): keep = lax.dynamic_index_in_dim(block_keep, holder, 0, False).reshape(-1)]
    pallas_call x0 -> x5, Pallas kernels: none -> 9.95 us  [the longest x1 3.3 us: shards(): call(functools.partial(scores_kernel, group), [vmem] * 6, [table, kv32, k...]
    ppermute x8, waiting for transfers between devices: 0.26 us -> 7.97 us  [from_behind(): lax.ppermute(block, axis, [((i - distance) % size, i) for i in range(size)])]
    convert_element_type x2 -> x0, other arithmetic: 3.48 us -> none  [the longest x1 1.74 us: shards(): value_sum.astype(jnp.bfloat16)]
    ppermute x8, starting transfers between devices: 15.6 us -> 12.5 us  [from_behind(): lax.ppermute(block, axis, [((i - distance) % size, i) for i in range(size)])]
    ppermute x2 -> x0, local copies, waits for them, and re-layouts: 2.04 us -> none  [from_behind(): return lax.ppermute(block, axis, route)]
    add x3 -> x0, local copies, waits for them, and re-layouts: 1.35 us -> none  [tile_mask(): key_pos = (key_order[:, None] * row_count + line[None, :]).reshape(-1)]
  transfers between devices with their start and end apart: 8 -> 8, of which waited for: 1 -> 3; matrix products, arithmetic and copies ran while one was open for 49% -> 4% of each run, Pallas kernels for 0% -> 16%
where the time goes in v1:
time: 36.2 us; the launch traced here: 35.9 us
  starting transfers between devices  12.5 us (35%)
  Pallas kernels  9.95 us (27%)
  waiting for transfers between devices  7.97 us (22%)
  local copies, waits for them, and re-layouts  4.7 us (13%)
  between operations  0.71 us (2%)
    ppermute x8, starting transfers between devices, from_behind(): lax.ppermute(block, axis, [((i - distance) % size, i) for i in range(size)])  12.5 us
    ppermute x8, waiting for transfers between devices, from_behind(): lax.ppermute(block, axis, [((i - distance) % size, i) for i in range(size)])  7.97 us
    unnamed x10, local copies, waits for them, and re-layouts  3.38 us
    pallas_call x1, Pallas kernels, shards(): call(functools.partial(scores_kernel, group), [vmem] * 6, [table, kv32, k...  3.3 us
    pallas_call x1, Pallas kernels, shards(): call(functools.partial(probs_kernel, group), [vmem] * 6, [table, kv32, kv...  3.14 us
    pallas_call x1, Pallas kernels, shards(): call(functools.partial(queries_kernel, group), [vmem] * 4, [rows], 1)  2.03 us
    dynamic_slice x1, local copies, waits for them, and re-layouts, shards(): lax.dynamic_index_in_dim(stretch_order, h, 0, False)  0.98 us
    pallas_call x1, Pallas kernels, shards(): call(add_kernel, [vmem] * 6, [kv16, kv16], 0)  0.74 us
  transfers between devices with their start and end apart: 8, of which 3 were waited for; matrix products, arithmetic and copies ran while one was open for 4% of the time, Pallas kernels for 16%

profile of v1, /device:TPU:1, one launch (start us, length us, event | category | flops | bytes accessed | tf_op | source)
XLA Modules:
  0.0 35.9 jit_solution(16707349754344955771)
XLA Ops:
  0.6 0.0 copy-start
  0.6 4.4 %collective-permute-start.2 = (bf16[128,512]{1,0:T(8,128)(2,1)}, bf16[128,512]{1,0:T(8,128)(2,1)S(1)}, u32[]{:S(2)}, u32[]{:S(2)}) collective-permute-start(bf16[128,512]{1,0:T(8,128)(2,1)} %vs.1), channel_id=1, source_target_pairs={{3,0},{0,1},{1,2},{2,3},{7,4},{4,5},{5,6},{6,7},{11,8},{8,9},{9,10... | collective-permute-start | bytes 393224 | tf_op jit(solution)/shard_map/ppermute | solution.py:26
  5.0 1.2 %collective-permute-start.3 = (bf16[128,512]{1,0:T(8,128)(2,1)}, bf16[128,512]{1,0:T(8,128)(2,1)S(1)}, u32[]{:S(2)}, u32[]{:S(2)}) collective-permute-start(bf16[128,512]{1,0:T(8,128)(2,1)} %vs.1), channel_id=1, source_target_pairs={{252,0},{0,4},{4,8},{8,12},{12,16},{16,20},{20,24},{24,28},{28,32}... | collective-permute-start | bytes 393224 | tf_op jit(solution)/shard_map/ppermute | solution.py:26
  6.2 1.2 %collective-permute-start.1 = (bf16[128,512]{1,0:T(8,128)(2,1)}, bf16[128,512]{1,0:T(8,128)(2,1)S(1)}, u32[]{:S(2)}, u32[]{:S(2)}) collective-permute-start(bf16[128,512]{1,0:T(8,128)(2,1)} %ks.3), channel_id=1, source_target_pairs={{252,0},{0,4},{4,8},{8,12},{12,16},{16,20},{20,24},{24,28},{28,32}... | collective-permute-start | bytes 393224 | tf_op jit(solution)/shard_map/ppermute | solution.py:26
  7.5 0.7 %collective-permute-start = (bf16[128,512]{1,0:T(8,128)(2,1)}, bf16[128,512]{1,0:T(8,128)(2,1)S(1)}, u32[]{:S(2)}, u32[]{:S(2)}) collective-permute-start(bf16[128,512]{1,0:T(8,128)(2,1)} %ks.3), channel_id=1, source_target_pairs={{3,0},{0,1},{1,2},{2,3},{7,4},{4,5},{5,6},{6,7},{11,8},{8,9},{9,10... | collective-permute-start | bytes 393224 | tf_op jit(solution)/shard_map/ppermute | solution.py:26
  8.1 0.0 copy-done
  8.1 0.3 dynamic-slice_reduce_fusion
  8.4 0.1 reshape.10
  8.5 1.0 %dynamic-slice_reduce_fusion.3 = (s32[2]{0:T(128)S(1)}, s32[2]{0:T(128)S(1)}, s32[2]{0:T(128)S(1)}) fusion(s32[256,2]{0,1:T(2,128)} %param.10, s32[]{:T(128)S(6)} %select_n.23, s32[]{:T(128)S(6)} %select_n.27, s32[]{:T(128)S(6)} %select_n.25), kind=kLoop, calls=%fused_computation.3 | loop fusion | bytes 60 | tf_op jit(solution)/shard_map/jit(dynamic_index_in_dim)/dynamic_slice | solution.py:137
  9.4 0.1 pad_add_fusion.meta
  9.5 0.0 copy-start.1
  9.5 1.2 %copy-done.1 = bf16[128,4096]{1,0:T(8,128)(2,1)S(1)} copy-done((bf16[128,4096]{1,0:T(8,128)(2,1)S(1)}, bf16[128,4096]{1,0:T(8,128)(2,1)}, u32[]{:S(2)}) %copy-start.1) | copy-done | bytes 1048600
  10.8 1.2 %copy-done.2 = bf16[128,4096]{1,0:T(8,128)(2,1)S(1)} copy-done((bf16[128,4096]{1,0:T(8,128)(2,1)S(1)}, bf16[128,4096]{1,0:T(8,128)(2,1)}, u32[]{:S(2)}) %copy-start.2) | copy-done | bytes 1048600
  12.0 0.7 %shard_map.85 = (bf16[128,4096]{1,0:T(8,128)(2,1)S(1)}, bf16[128,4096]{1,0:T(8,128)(2,1)S(1)}, f32[384,128]{1,0:T(8,128)S(1)}) custom-call(s32[18]{0:T(128)S(1)} %pad_add_fusion.meta, bf16[128,4096]{1,0:T(8,128)(2,1)S(1)} %copy-done.1, bf16[128,4096]{1,0:T(8,128)(2,1)S(1)} %copy-done.2), custom_call_target="tpu_custom_call" | custom-call | flops 402653184 | bytes 1048576 | tf_op jit(solution)/shard_map/pallas_call | solution.py:162
  12.7 5.3 %collective-permute-done.1.ko = bf16[128,512]{1,0:T(8,128)(2,1)S(1)} collective-permute-done((bf16[128,512]{1,0:T(8,128)(2,1)}, bf16[128,512]{1,0:T(8,128)(2,1)S(1)}, u32[]{:S(2)}, u32[]{:S(2)}) %collective-permute-start.1) | collective-permute-done | bytes 131104 | tf_op jit(solution)/shard_map/ppermute | solution.py:26
  18.1 0.0 collective-permute-done.ki
  18.1 0.9 %copy-done.4 = bf16[128,512]{1,0:T(8,128)(2,1)S(1)} copy-done((bf16[128,512]{1,0:T(8,128)(2,1)S(1)}, bf16[128,512]{1,0:T(8,128)(2,1)}, u32[]{:S(2)}) %copy-start.4) | copy-done | bytes 131096
  19.0 3.1 %shard_map.86 = (bf16[4,384,1024]{2,1,0:T(8,128)(2,1)S(1)}, f32[128,512]{1,0:T(8,128)S(1)}, bf16[128,512]{1,0:T(8,128)(2,1)S(1)}, bf16[128,512]{1,0:T(8,128)(2,1)S(1)}) custom-call(f32[384,128]{1,0:T(8,128)S(1)} %get-tuple-element.18.bias, bf16[128,4096]{1,0:T(8,128)(2,1)S(1)} %get-tuple-element.16.q, bf16[128,4096]{1,0:T(8,128)(2,1)S(1)} %get-tuple-element.17.g, ...), custom_call_target="tpu_custom_call" | custom-call | flops 805306368 | bytes 1048576 | tf_op jit(solution)/shard_map/pallas_call | solution.py:169
  22.1 0.0 collective-permute-done.2.vi
  22.1 0.0 collective-permute-done.3.vo
  22.1 0.0 copy-done.3
  22.2 3.3 %shard_map.87 = (bf16[4,384,1024]{2,1,0:T(8,128)(2,1)S(1)}, f32[128,512]{1,0:T(8,128)S(1)}, bf16[128,512]{1,0:T(8,128)(2,1)S(1)}, bf16[128,512]{1,0:T(8,128)(2,1)S(1)}) custom-call(bf16[128,4096]{1,0:T(8,128)(2,1)S(1)} %get-tuple-element.16.q, bf16[128,4096]{1,0:T(8,128)(2,1)S(1)} %get-tuple-element.17.g, bf16[128,512]{1,0:T(8,128)(2,1)S(1)} %copy-done.3, ...), custom_call_target="tpu_custom_call" | custom-call | flops 805306368 | bytes 1048576 | tf_op jit(solution)/shard_map/pallas_call | solution.py:174
  25.5 0.1 collective-permute-start.4
  25.5 1.8 %collective-permute-start.5 = (bf16[128,512]{1,0:T(8,128)(2,1)S(1)}, bf16[128,512]{1,0:T(8,128)(2,1)S(1)}, u32[]{:S(2)}, u32[]{:S(2)}) collective-permute-start(bf16[128,512]{1,0:T(8,128)(2,1)S(1)} %get-tuple-element.23), channel_id=1, source_target_pairs={{4,0},{8,4},{12,8},{16,12},{20,16},{24,20},{28,24},{32,28},{36,32}... | collective-permute-start | bytes 393224 | tf_op jit(solution)/shard_map/ppermute | solution.py:26
  27.4 2.6 %collective-permute-start.6 = (bf16[128,512]{1,0:T(8,128)(2,1)S(1)}, bf16[128,512]{1,0:T(8,128)(2,1)S(1)}, u32[]{:S(2)}, u32[]{:S(2)}) collective-permute-start(bf16[128,512]{1,0:T(8,128)(2,1)S(1)} %get-tuple-element.25), channel_id=1, source_target_pairs={{1,0},{2,1},{3,2},{0,3},{5,4},{6,5},{7,6},{4,7},{9,8},{10,9},{11,1... | collective-permute-start | bytes 393224 | tf_op jit(solution)/shard_map/ppermute | solution.py:26
  30.0 0.5 %collective-permute-start.7 = (bf16[128,512]{1,0:T(8,128)(2,1)S(1)}, bf16[128,512]{1,0:T(8,128)(2,1)S(1)}, u32[]{:S(2)}, u32[]{:S(2)}) collective-permute-start(bf16[128,512]{1,0:T(8,128)(2,1)S(1)} %get-tuple-element.26), channel_id=1, source_target_pairs={{4,0},{8,4},{12,8},{16,12},{20,16},{24,20},{28,24},{32,28},{36,32}... | collective-permute-start | bytes 393224 | tf_op jit(solution)/shard_map/ppermute | solution.py:26
  30.5 2.0 %shard_map.88 = bf16[128,4096]{1,0:T(8,128)(2,1)} custom-call(bf16[128,512]{1,0:T(8,128)(2,1)S(1)} %copy-done.4, bf16[128,512]{1,0:T(8,128)(2,1)S(1)} %collective-permute-done.ki, bf16[128,512]{1,0:T(8,128)(2,1)S(1)} %collective-permute-done.1.ko, bf16[4,384,1024]{2,1,0:T(8,128)(2,1)S(1)} %get-tuple-element.20.dscores), custom_call_target="tpu_custom_call" | custom-call | flops 402653184 | bytes 1048576 | tf_op jit(solution)/shard_map/pallas_call | solution.py:179
  32.5 0.0 collective-permute-done.4.b
  32.5 0.0 collective-permute-done.5.c
  32.6 1.5 %collective-permute-done.6.e = bf16[128,512]{1,0:T(8,128)(2,1)S(1)} collective-permute-done((bf16[128,512]{1,0:T(8,128)(2,1)S(1)}, bf16[128,512]{1,0:T(8,128)(2,1)S(1)}, u32[]{:S(2)}, u32[]{:S(2)}) %collective-permute-start.6) | collective-permute-done | bytes 131104 | tf_op jit(solution)/shard_map/ppermute | solution.py:26
  34.1 1.1 %collective-permute-done.7.f = bf16[128,512]{1,0:T(8,128)(2,1)S(1)} collective-permute-done((bf16[128,512]{1,0:T(8,128)(2,1)S(1)}, bf16[128,512]{1,0:T(8,128)(2,1)S(1)}, u32[]{:S(2)}, u32[]{:S(2)}) %collective-permute-start.7) | collective-permute-done | bytes 131104 | tf_op jit(solution)/shard_map/ppermute | solution.py:26
  35.2 0.7 %shard_map.89 = (bf16[128,512]{1,0:T(8,128)(2,1)}, bf16[128,512]{1,0:T(8,128)(2,1)}) custom-call(f32[128,512]{1,0:T(8,128)S(1)} %get-tuple-element.21.a, bf16[128,512]{1,0:T(8,128)(2,1)S(1)} %collective-permute-done.4.b, bf16[128,512]{1,0:T(8,128)(2,1)S(1)} %collective-permute-done.5.c, f32[128,512]{1,0:T(8,128)S(1)} %get-tuple-element.24.d, ...), custom_call_target="tpu_custom_call" | custom-call | bytes 1048576 | tf_op jit(solution)/shard_map/pallas_call | solution.py:180
  (3 shorter events, 0.0 us)
Async XLA Ops:
  0.6 7.5 %copy-start = (s32[256,3,2,2]{0,3,2,1:T(2,128)S(1)}, s32[256,3,2,2]{0,3,2,1:T(2,128)}, u32[]{:S(2)}) copy-start(s32[256,3,2,2]{0,3,2,1:T(2,128)} %param.11) | copy-start | bytes 36868
  0.6 21.5 %collective-permute-start.2 = (bf16[128,512]{1,0:T(8,128)(2,1)}, bf16[128,512]{1,0:T(8,128)(2,1)S(1)}, u32[]{:S(2)}, u32[]{:S(2)}) collective-permute-start(bf16[128,512]{1,0:T(8,128)(2,1)} %vs.1), channel_id=1, source_target_pairs={{3,0},{0,1},{1,2},{2,3},{7,4},{4,5},{5,6},{6,7},{11,8},{8,9},{9,10... | collective-permute-start | bytes 393224 | tf_op jit(solution)/shard_map/ppermute | solution.py:26
  5.0 17.1 %collective-permute-start.3 = (bf16[128,512]{1,0:T(8,128)(2,1)}, bf16[128,512]{1,0:T(8,128)(2,1)S(1)}, u32[]{:S(2)}, u32[]{:S(2)}) collective-permute-start(bf16[128,512]{1,0:T(8,128)(2,1)} %vs.1), channel_id=1, source_target_pairs={{252,0},{0,4},{4,8},{8,12},{12,16},{16,20},{20,24},{24,28},{28,32}... | collective-permute-start | bytes 393224 | tf_op jit(solution)/shard_map/ppermute | solution.py:26
  6.2 11.8 %collective-permute-start.1 = (bf16[128,512]{1,0:T(8,128)(2,1)}, bf16[128,512]{1,0:T(8,128)(2,1)S(1)}, u32[]{:S(2)}, u32[]{:S(2)}) collective-permute-start(bf16[128,512]{1,0:T(8,128)(2,1)} %ks.3), channel_id=1, source_target_pairs={{252,0},{0,4},{4,8},{8,12},{12,16},{16,20},{20,24},{24,28},{28,32}... | collective-permute-start | bytes 393224 | tf_op jit(solution)/shard_map/ppermute | solution.py:26
  7.5 10.6 %collective-permute-start = (bf16[128,512]{1,0:T(8,128)(2,1)}, bf16[128,512]{1,0:T(8,128)(2,1)S(1)}, u32[]{:S(2)}, u32[]{:S(2)}) collective-permute-start(bf16[128,512]{1,0:T(8,128)(2,1)} %ks.3), channel_id=1, source_target_pairs={{3,0},{0,1},{1,2},{2,3},{7,4},{4,5},{5,6},{6,7},{11,8},{8,9},{9,10... | collective-permute-start | bytes 393224 | tf_op jit(solution)/shard_map/ppermute | solution.py:26
  9.5 1.2 %copy-start.1 = (bf16[128,4096]{1,0:T(8,128)(2,1)S(1)}, bf16[128,4096]{1,0:T(8,128)(2,1)}, u32[]{:S(2)}) copy-start(bf16[128,4096]{1,0:T(8,128)(2,1)} %queries.1) | copy-start | bytes 3145732
  10.8 1.2 %copy-start.2 = (bf16[128,4096]{1,0:T(8,128)(2,1)S(1)}, bf16[128,4096]{1,0:T(8,128)(2,1)}, u32[]{:S(2)}) copy-start(bf16[128,4096]{1,0:T(8,128)(2,1)} %grads.1) | copy-start | bytes 3145732
  12.0 10.2 %copy-start.3 = (bf16[128,512]{1,0:T(8,128)(2,1)S(1)}, bf16[128,512]{1,0:T(8,128)(2,1)}, u32[]{:S(2)}) copy-start(bf16[128,512]{1,0:T(8,128)(2,1)} %vs.1) | copy-start | bytes 393220
  18.1 0.9 %copy-start.4 = (bf16[128,512]{1,0:T(8,128)(2,1)S(1)}, bf16[128,512]{1,0:T(8,128)(2,1)}, u32[]{:S(2)}) copy-start(bf16[128,512]{1,0:T(8,128)(2,1)} %ks.3) | copy-start | bytes 393220
  25.5 7.1 %collective-permute-start.4 = (bf16[128,512]{1,0:T(8,128)(2,1)S(1)}, bf16[128,512]{1,0:T(8,128)(2,1)S(1)}, u32[]{:S(2)}, u32[]{:S(2)}) collective-permute-start(bf16[128,512]{1,0:T(8,128)(2,1)S(1)} %get-tuple-element.22), channel_id=1, source_target_pairs={{1,0},{2,1},{3,2},{0,3},{5,4},{6,5},{7,6},{4,7},{9,8},{10,9},{11,1... | collective-permute-start | bytes 393224 | tf_op jit(solution)/shard_map/ppermute | solution.py:26
  25.5 7.0 %collective-permute-start.5 = (bf16[128,512]{1,0:T(8,128)(2,1)S(1)}, bf16[128,512]{1,0:T(8,128)(2,1)S(1)}, u32[]{:S(2)}, u32[]{:S(2)}) collective-permute-start(bf16[128,512]{1,0:T(8,128)(2,1)S(1)} %get-tuple-element.23), channel_id=1, source_target_pairs={{4,0},{8,4},{12,8},{16,12},{20,16},{24,20},{28,24},{32,28},{36,32}... | collective-permute-start | bytes 393224 | tf_op jit(solution)/shard_map/ppermute | solution.py:26
  27.4 6.7 %collective-permute-start.6 = (bf16[128,512]{1,0:T(8,128)(2,1)S(1)}, bf16[128,512]{1,0:T(8,128)(2,1)S(1)}, u32[]{:S(2)}, u32[]{:S(2)}) collective-permute-start(bf16[128,512]{1,0:T(8,128)(2,1)S(1)} %get-tuple-element.25), channel_id=1, source_target_pairs={{1,0},{2,1},{3,2},{0,3},{5,4},{6,5},{7,6},{4,7},{9,8},{10,9},{11,1... | collective-permute-start | bytes 393224 | tf_op jit(solution)/shard_map/ppermute | solution.py:26
  30.0 5.2 %collective-permute-start.7 = (bf16[128,512]{1,0:T(8,128)(2,1)S(1)}, bf16[128,512]{1,0:T(8,128)(2,1)S(1)}, u32[]{:S(2)}, u32[]{:S(2)}) collective-permute-start(bf16[128,512]{1,0:T(8,128)(2,1)S(1)} %get-tuple-element.26), channel_id=1, source_target_pairs={{4,0},{8,4},{12,8},{16,12},{20,16},{24,20},{28,24},{32,28},{36,32}... | collective-permute-start | bytes 393224 | tf_op jit(solution)/shard_map/ppermute | solution.py:26

commit v2 on v1

--- a/solution.py
+++ b/solution.py
@@ -55,22 +55,25 @@
             bias[row : row + stretch, :] = jnp.where(allowed, 0.0, NEG_BIG)
 
 
-def stage_kernel(meta, queries, grads, q, g, bias, sems):
+def stage_kernel(queries, grads, keys, values, q, g, k, v, sems):
     copies = [
-        pltpu.make_async_copy(queries, q, sems.at[0]),
-        pltpu.make_async_copy(grads, g, sems.at[1]),
+        pltpu.make_async_copy(source, target, sems.at[n])
+        for n, (source, target) in enumerate(((queries, q), (grads, g), (keys, k), (values, v)))
     ]
     for copy in copies:
         copy.start()
-    fill_bias(meta, bias, bias.shape[1] // 2)
     for copy in copies:
         copy.wait()
 
 
-def probs_kernel(group, bias, q, g, ks, ki, ko, probs, dvs, dvi, dvo):
+def bias_kernel(meta, bias):
+    fill_bias(meta, bias, bias.shape[1] // 2)
+
+
+def probs_kernel(group, bias, q, g, ks, ki, ko, probs, dvs, dvi, dvo, work):
     span = q.shape[0]
+    outs = []
     for h in range(ks.shape[1] // HEAD_DIM):
-        lanes = slice(h * HEAD_DIM, (h + 1) * HEAD_DIM)
         keys = stack_sources((ks, ki, ko), h)
         for pair in range(group // 2):
             cols = slice(2 * pair * HEAD_DIM, (2 * pair + 2) * HEAD_DIM)
@@ -80,42 +83,50 @@
             peak = jnp.max(scores, axis=0, keepdims=True)
             raised = jnp.exp2(scores - peak)
             total = jnp.sum(raised, axis=0, keepdims=True)
-            probs[h, :, cols] = (raised * (1.0 / total)).astype(jnp.bfloat16)
-        out = dot(probs[h], stack_heads(g, h * group, group), NN)
+            work[h, :, cols] = (raised * (1.0 / total)).astype(jnp.bfloat16)
+        outs.append(dot(work[h], stack_heads(g, h * group, group), NN))
+    for h, out in enumerate(outs):
+        lanes = slice(h * HEAD_DIM, (h + 1) * HEAD_DIM)
         dvs[:, lanes] = out[:span]
         dvi[:, lanes] = out[span : 2 * span].astype(jnp.bfloat16)
         dvo[:, lanes] = out[2 * span :].astype(jnp.bfloat16)
-
-
-def scores_kernel(group, q, g, vs, vi, vo, probs, dscores, dks, dki, dko):
+    probs[...] = work[...]
+
+
+def scores_kernel(group, q, g, vs, vi, vo, probs, dscores, dks, dki, dko, work):
     span = q.shape[0]
+    outs = []
     for h in range(vs.shape[1] // HEAD_DIM):
-        lanes = slice(h * HEAD_DIM, (h + 1) * HEAD_DIM)
         values = stack_sources((vs, vi, vo), h)
         for pair in range(group // 2):
             cols = slice(2 * pair * HEAD_DIM, (2 * pair + 2) * HEAD_DIM)
             grad_probs = dot(values, stack_heads(g, h * group + 2 * pair, 2), NT)
             weight = probs[h, :, cols].astype(jnp.float32)
             delta = jnp.sum(weight * grad_probs, axis=0, keepdims=True)
-            dscores[h, :, cols] = (weight * ((grad_probs - delta) * SCALE)).astype(jnp.bfloat16)
-        out = dot(dscores[h], stack_heads(q, h * group, group), NN)
+            work[h, :, cols] = (weight * ((grad_probs - delta) * SCALE)).astype(jnp.bfloat16)
+        outs.append(dot(work[h], stack_heads(q, h * group, group), NN))
+    for h, out in enumerate(outs):
+        lanes = slice(h * HEAD_DIM, (h + 1) * HEAD_DIM)
         dks[:, lanes] = out[:span]
         dki[:, lanes] = out[span : 2 * span].astype(jnp.bfloat16)
         dko[:, lanes] = out[2 * span :].astype(jnp.bfloat16)
-
-
-def queries_kernel(group, ks, ki, ko, dscores, dq):
+    dscores[...] = work[...]
+
+
+def queries_kernel(group, ks, ki, ko, dscores, dvs, dvi, dvo, dq, dv):
+    dv[...] = (dvs[...] + dvi[...].astype(jnp.float32) + dvo[...].astype(jnp.float32)).astype(dv.dtype)
+    outs = []
     for h in range(ks.shape[1] // HEAD_DIM):
         keys = stack_sources((ks, ki, ko), h)
+        outs.append(dot(keys, dscores[h], TN).astype(jnp.bfloat16))
+    for h, out in enumerate(outs):
         for g in range(group):
             lanes = slice((h * group + g) * HEAD_DIM, (h * group + g + 1) * HEAD_DIM)
-            cols = slice(g * HEAD_DIM, (g + 1) * HEAD_DIM)
-            dq[:, lanes] = dot(dscores[h, :, cols], keys, TN).astype(jnp.bfloat16)
-
-
-def add_kernel(a, b, c, d, e, f, dk, dv):
-    dk[...] = (a[...] + b[...].astype(jnp.float32) + c[...].astype(jnp.float32)).astype(dk.dtype)
-    dv[...] = (d[...] + e[...].astype(jnp.float32) + f[...].astype(jnp.float32)).astype(dv.dtype)
+            dq[:, lanes] = out[:, g * HEAD_DIM : (g + 1) * HEAD_DIM].T
+
+
+def add_kernel(a, b, c, out):
+    out[...] = (a[...] + b[...].astype(jnp.float32) + c[...].astype(jnp.float32)).astype(out.dtype)
 
 
 def shards(queries, keys, values, grad_out, stretch_order, block_keep):
@@ -132,8 +143,6 @@
     outer_prev = (pos_outer + n_outer - 1) % n_outer * n_inner + pos_inner
     k_out = from_behind(keys, "outer", 1)
     k_in = from_behind(keys, "inner", 1)
-    v_out = from_behind(values, "outer", 1)
-    v_in = from_behind(values, "inner", 1)
     orders = [lax.dynamic_index_in_dim(stretch_order, h, 0, False) for h in (holder, inner_prev, outer_prev)]
     keep = lax.dynamic_index_in_dim(block_keep, holder, 0, False).reshape(-1)
     meta = jnp.concatenate(orders + [keep])
@@ -141,14 +150,14 @@
     f32, bf16 = jnp.float32, jnp.bfloat16
     vmem = pl.BlockSpec(memory_space=pltpu.VMEM)
     smem = pl.BlockSpec(memory_space=pltpu.SMEM)
-    hbm = pl.BlockSpec(memory_space=pl.ANY)
+    hbm = pl.BlockSpec(memory_space=pltpu.HBM)
     rows = jax.ShapeDtypeStruct(queries.shape, bf16)
     table = jax.ShapeDtypeStruct((kv_heads, 3 * span, group * HEAD_DIM), bf16)
     kv32 = jax.ShapeDtypeStruct((span, width), f32)
     kv16 = jax.ShapeDtypeStruct((span, width), bf16)
     flops = 2 * span * queries.shape[1] * 3 * span
 
-    def call(kernel, ins, out_shape, ops, scratch=()):
+    def call(kernel, ins, out_shape, ops, scratch=(), size=2**20):
         return pl.pallas_call(
             kernel,
             in_specs=ins,
@@ -156,28 +165,31 @@
             out_shape=out_shape,
             scratch_shapes=scratch,
             compiler_params=pltpu.CompilerParams(vmem_limit_bytes=VMEM),
-            cost_estimate=pl.CostEstimate(flops=ops * flops, bytes_accessed=2**20, transcendentals=0),
+            cost_estimate=pl.CostEstimate(flops=ops * flops, bytes_accessed=size, transcendentals=0),
         )
 
-    q, g, bias = call(
-        stage_kernel,
-        [smem, hbm, hbm],
-        [rows, rows, jax.ShapeDtypeStruct((3 * span, span), f32)],
-        1,
-        [pltpu.SemaphoreType.DMA((2,))],
-    )(meta, queries, grad_out)
+    q, g, k, v = call(stage_kernel, [hbm] * 4, [rows, rows, kv16, kv16], 0, [pltpu.SemaphoreType.DMA((4,))])(
+        *(pltpu.with_memory_space_constraint(x, pltpu.HBM) for x in (queries, grad_out, keys, values))
+    )
+    v_out = from_behind(values, "outer", 1)
+    v_in = from_behind(values, "inner", 1)
+    (bias,) = call(bias_kernel, [smem], [jax.ShapeDtypeStruct((3 * span, span), f32)], 0)(meta)
+    work = [pltpu.VMEM(table.shape, bf16)]
     probs, dvs, dvi, dvo = call(
-        functools.partial(probs_kernel, group), [vmem] * 6, [table, kv32, kv16, kv16], 2
-    )(bias, q, g, keys, k_in, k_out)
+        functools.partial(probs_kernel, group), [vmem] * 6, [table, kv32, kv16, kv16], 2, work
+    )(bias, q, g, k, k_in, k_out)
     dv_out = from_behind(dvo, "outer", -1)
     dv_in = from_behind(dvi, "inner", -1)
     dscores, dks, dki, dko = call(
-        functools.partial(scores_kernel, group), [vmem] * 6, [table, kv32, kv16, kv16], 2
-    )(q, g, values, v_in, v_out, probs)
+        functools.partial(scores_kernel, group), [vmem] * 6, [table, kv32, kv16, kv16], 2, work
+    )(q, g, v, v_in, v_out, probs)
     dk_out = from_behind(dko, "outer", -1)
     dk_in = from_behind(dki, "inner", -1)
-    (dq,) = call(functools.partial(queries_kernel, group), [vmem] * 4, [rows], 1)(keys, k_in, k_out, dscores)
-    dk, dv = call(add_kernel, [vmem] * 6, [kv16, kv16], 0)(dks, dk_in, dk_out, dvs, dv_in, dv_out)
+    dq, dv = call(functools.partial(queries_kernel, group), [vmem] * 7, [rows, kv16], 1)(
+        k, k_in, k_out, dscores, dvs, dv_in, dv_out
+    )
+    dks, dq, dv = lax.optimization_barrier((dks, dq, dv))
+    (dk,) = call(add_kernel, [vmem] * 3, [kv16], 0)(dks, dk_in, dk_out)
     return dq, dk, dv
 
 

time: 36.2 us -> 30.1 us (0.83)
  waiting for transfers between devices: 7.97 us -> 3.81 us
  local copies, waits for them, and re-layouts: 4.7 us -> 1.33 us
  starting transfers between devices: 12.5 us -> 13.9 us
    ppermute x8, waiting for transfers between devices: 7.97 us -> 3.81 us  [from_behind(): lax.ppermute(block, axis, [((i - distance) % size, i) for i in range(size)])]
    unnamed x10 -> x2, local copies, waits for them, and re-layouts: 3.38 us -> 0.01 us
    ppermute x8, starting transfers between devices: 12.5 us -> 13.9 us  [from_behind(): lax.ppermute(block, axis, [((i - distance) % size, i) for i in range(size)])]
    pallas_call x3 -> x4, Pallas kernels: 3.52 us -> 4.73 us  [the longest x1 1.84 us: shards(): call(functools.partial(queries_kernel, group), [vmem] * 7, [rows, kv16], 1)]
    pallas_call x1, Pallas kernels: 3.14 us -> 2.58 us  [shards(): call(functools.partial(probs_kernel, group), [vmem] * 6, [table, kv32, kv...]
    pallas_call x1, Pallas kernels: 3.3 us -> 2.83 us  [shards(): call(functools.partial(scores_kernel, group), [vmem] * 6, [table, kv32, k...]
  transfers between devices with their start and end apart: 8 -> 8, of which waited for: 3 -> 2; matrix products, arithmetic and copies ran while one was open for 4% -> 5% of each run, Pallas kernels for 16% -> 32%
where the time goes in v2:
time: 30.1 us; the launch traced here: 29.9 us
  starting transfers between devices  13.9 us (46%)
  Pallas kernels  10.2 us (34%)
  waiting for transfers between devices  3.81 us (13%)
  local copies, waits for them, and re-layouts  1.33 us (4%)
  between operations  0.68 us (2%)
    ppermute x8, starting transfers between devices, from_behind(): lax.ppermute(block, axis, [((i - distance) % size, i) for i in range(size)])  13.9 us
    ppermute x8, waiting for transfers between devices, from_behind(): lax.ppermute(block, axis, [((i - distance) % size, i) for i in range(size)])  3.81 us
    pallas_call x1, Pallas kernels, shards(): call(functools.partial(scores_kernel, group), [vmem] * 6, [table, kv32, k...  2.83 us
    pallas_call x1, Pallas kernels, shards(): call(functools.partial(probs_kernel, group), [vmem] * 6, [table, kv32, kv...  2.58 us
    pallas_call x1, Pallas kernels, shards(): call(functools.partial(queries_kernel, group), [vmem] * 7, [rows, kv16], 1)  1.84 us
    pallas_call x1, Pallas kernels, shards(): call(stage_kernel, [hbm] * 4, [rows, rows, kv16, kv16], 0, [pltpu.Semapho...  1.61 us
    dynamic_slice x1, local copies, waits for them, and re-layouts, shards(): lax.dynamic_index_in_dim(stretch_order, h, 0, False)  0.98 us
    pallas_call x1, Pallas kernels, shards(): dk, = call(add_kernel, [vmem] * 3, [kv16], 0)(dks, dk_in, dk_out)  0.7 us
  transfers between devices with their start and end apart: 8, of which 2 were waited for; matrix products, arithmetic and copies ran while one was open for 5% of the time, Pallas kernels for 32%

profile of v2, /device:TPU:1, one launch (start us, length us, event | category | flops | bytes accessed | tf_op | source)
XLA Modules:
  0.0 29.9 jit_solution(9798088845288485459)
XLA Ops:
  0.6 0.0 copy-start
  0.6 2.1 %collective-permute-start.3 = (bf16[128,512]{1,0:T(8,128)(2,1)}, bf16[128,512]{1,0:T(8,128)(2,1)S(1)}, u32[]{:S(2)}, u32[]{:S(2)}) collective-permute-start(bf16[128,512]{1,0:T(8,128)(2,1)} %keys.1), channel_id=1, source_target_pairs={{252,0},{0,4},{4,8},{8,12},{12,16},{16,20},{20,24},{24,28},{28,32}... | collective-permute-start | bytes 393224 | tf_op jit(solution)/shard_map/ppermute | solution.py:26
  2.8 3.8 %collective-permute-start.2 = (bf16[128,512]{1,0:T(8,128)(2,1)}, bf16[128,512]{1,0:T(8,128)(2,1)S(1)}, u32[]{:S(2)}, u32[]{:S(2)}) collective-permute-start(bf16[128,512]{1,0:T(8,128)(2,1)} %keys.1), channel_id=1, source_target_pairs={{3,0},{0,1},{1,2},{2,3},{7,4},{4,5},{5,6},{6,7},{11,8},{8,9},{9,10... | collective-permute-start | bytes 393224 | tf_op jit(solution)/shard_map/ppermute | solution.py:26
  6.5 1.2 %collective-permute-start.1 = (bf16[128,512]{1,0:T(8,128)(2,1)}, bf16[128,512]{1,0:T(8,128)(2,1)S(1)}, u32[]{:S(2)}, u32[]{:S(2)}) collective-permute-start(bf16[128,512]{1,0:T(8,128)(2,1)} %values.1), channel_id=1, source_target_pairs={{252,0},{0,4},{4,8},{8,12},{12,16},{16,20},{20,24},{24,28},{28,32}... | collective-permute-start | bytes 393224 | tf_op jit(solution)/shard_map/ppermute | solution.py:26
  7.7 0.3 collective-permute-start
  8.0 0.0 copy-done
  8.0 0.3 dynamic-slice_reduce_fusion
  8.3 0.1 reshape.10
  8.4 1.0 %dynamic-slice_reduce_fusion.3 = (s32[2]{0:T(128)S(1)}, s32[2]{0:T(128)S(1)}, s32[2]{0:T(128)S(1)}) fusion(s32[256,2]{0,1:T(2,128)} %param.10, s32[]{:T(128)S(6)} %select_n.23, s32[]{:T(128)S(6)} %select_n.27, s32[]{:T(128)S(6)} %select_n.25), kind=kLoop, calls=%fused_computation.3 | loop fusion | bytes 60 | tf_op jit(solution)/shard_map/jit(dynamic_index_in_dim)/dynamic_slice | solution.py:146
  9.3 0.1 pad_add_fusion.meta
  9.4 0.6 %shard_map.86.bias = f32[384,128]{1,0:T(8,128)S(1)} custom-call(s32[18]{0:T(128)S(1)} %pad_add_fusion.meta), custom_call_target="tpu_custom_call" | custom-call | bytes 1048576 | tf_op jit(solution)/shard_map/pallas_call | solution.py:176
  10.0 1.6 %shard_map.85 = (bf16[128,4096]{1,0:T(8,128)(2,1)S(1)}, bf16[128,4096]{1,0:T(8,128)(2,1)S(1)}, bf16[128,512]{1,0:T(8,128)(2,1)S(1)}, bf16[128,512]{1,0:T(8,128)(2,1)S(1)}) custom-call(bf16[128,4096]{1,0:T(8,128)(2,1)} %queries.1, bf16[128,4096]{1,0:T(8,128)(2,1)} %grads.1, bf16[128,512]{1,0:T(8,128)(2,1)} %keys.1, bf16[128,512]{1,0:T(8,128)(2,1)} %values.1), custom_call_target="tpu_custom_call" | custom-call | bytes 1048576 | tf_op jit(solution)/shard_map/pallas_call | solution.py:171
  11.6 2.1 %collective-permute-done.3.ko = bf16[128,512]{1,0:T(8,128)(2,1)S(1)} collective-permute-done((bf16[128,512]{1,0:T(8,128)(2,1)}, bf16[128,512]{1,0:T(8,128)(2,1)S(1)}, u32[]{:S(2)}, u32[]{:S(2)}) %collective-permute-start.3) | collective-permute-done | bytes 131104 | tf_op jit(solution)/shard_map/ppermute | solution.py:26
  13.8 0.0 collective-permute-done.2.ki
  13.8 2.6 %shard_map.87 = (bf16[4,384,1024]{2,1,0:T(8,128)(2,1)S(1)}, f32[128,512]{1,0:T(8,128)S(1)}, bf16[128,512]{1,0:T(8,128)(2,1)S(1)}, bf16[128,512]{1,0:T(8,128)(2,1)S(1)}) custom-call(f32[384,128]{1,0:T(8,128)S(1)} %shard_map.86.bias, bf16[128,4096]{1,0:T(8,128)(2,1)S(1)} %get-tuple-element.20.q, bf16[128,4096]{1,0:T(8,128)(2,1)S(1)} %get-tuple-element.21.g, ...), custom_call_target="tpu_custom_call" | custom-call | flops 805306368 | bytes 1048576 | tf_op jit(solution)/shard_map/pallas_call | solution.py:178
  16.4 1.4 %collective-permute-start.4 = (bf16[128,512]{1,0:T(8,128)(2,1)S(1)}, bf16[128,512]{1,0:T(8,128)(2,1)S(1)}, u32[]{:S(2)}, u32[]{:S(2)}) collective-permute-start(bf16[128,512]{1,0:T(8,128)(2,1)S(1)} %get-tuple-element.28), channel_id=1, source_target_pairs={{1,0},{2,1},{3,2},{0,3},{5,4},{6,5},{7,6},{4,7},{9,8},{10,9},{11,1... | collective-permute-start | bytes 393224 | tf_op jit(solution)/shard_map/ppermute | solution.py:26
  17.7 2.1 %collective-permute-start.5 = (bf16[128,512]{1,0:T(8,128)(2,1)S(1)}, bf16[128,512]{1,0:T(8,128)(2,1)S(1)}, u32[]{:S(2)}, u32[]{:S(2)}) collective-permute-start(bf16[128,512]{1,0:T(8,128)(2,1)S(1)} %get-tuple-element.29), channel_id=1, source_target_pairs={{4,0},{8,4},{12,8},{16,12},{20,16},{24,20},{28,24},{32,28},{36,32}... | collective-permute-start | bytes 393224 | tf_op jit(solution)/shard_map/ppermute | solution.py:26
  19.9 0.0 collective-permute-done.1.vo
  19.9 0.0 collective-permute-done.vi
  19.9 2.8 %shard_map.88 = (bf16[4,384,1024]{2,1,0:T(8,128)(2,1)S(1)}, f32[128,512]{1,0:T(8,128)S(1)}, bf16[128,512]{1,0:T(8,128)(2,1)S(1)}, bf16[128,512]{1,0:T(8,128)(2,1)S(1)}) custom-call(bf16[128,4096]{1,0:T(8,128)(2,1)S(1)} %get-tuple-element.20.q, bf16[128,4096]{1,0:T(8,128)(2,1)S(1)} %get-tuple-element.21.g, bf16[128,512]{1,0:T(8,128)(2,1)S(1)} %get-tuple-element.22.vs, ...), custom_call_target="tpu_custom_call" | custom-call | flops 805306368 | bytes 1048576 | tf_op jit(solution)/shard_map/pallas_call | solution.py:183
  22.7 1.4 %collective-permute-start.6 = (bf16[128,512]{1,0:T(8,128)(2,1)S(1)}, bf16[128,512]{1,0:T(8,128)(2,1)S(1)}, u32[]{:S(2)}, u32[]{:S(2)}) collective-permute-start(bf16[128,512]{1,0:T(8,128)(2,1)S(1)} %get-tuple-element.34), channel_id=1, source_target_pairs={{1,0},{2,1},{3,2},{0,3},{5,4},{6,5},{7,6},{4,7},{9,8},{10,9},{11,1... | collective-permute-start | bytes 393224 | tf_op jit(solution)/shard_map/ppermute | solution.py:26
  24.1 1.7 %collective-permute-start.7 = (bf16[128,512]{1,0:T(8,128)(2,1)S(1)}, bf16[128,512]{1,0:T(8,128)(2,1)S(1)}, u32[]{:S(2)}, u32[]{:S(2)}) collective-permute-start(bf16[128,512]{1,0:T(8,128)(2,1)S(1)} %get-tuple-element.35), channel_id=1, source_target_pairs={{4,0},{8,4},{12,8},{16,12},{20,16},{24,20},{28,24},{32,28},{36,32}... | collective-permute-start | bytes 393224 | tf_op jit(solution)/shard_map/ppermute | solution.py:26
  25.7 0.0 collective-permute-done.4.dvi
  25.7 0.0 collective-permute-done.5.dvo
  25.7 1.8 %shard_map.89 = (bf16[128,4096]{1,0:T(8,128)(2,1)}, bf16[128,512]{1,0:T(8,128)(2,1)}) custom-call(bf16[128,512]{1,0:T(8,128)(2,1)S(1)} %get-tuple-element.23.ks, bf16[128,512]{1,0:T(8,128)(2,1)S(1)} %collective-permute-done.2.ki, bf16[128,512]{1,0:T(8,128)(2,1)S(1)} %collective-permute-done.3.ko, bf16[4,384,1024]{2,1,0:T(8,128)(2,1)S(1)} %get-tuple-element.26.dscores, ...), custom_call_target="tpu_custom_call" | custom-call | flops 402653184 | bytes 1048576 | tf_op jit(solution)/shard_map/pallas_call | solution.py:188
  27.6 1.7 %collective-permute-done.6.b = bf16[128,512]{1,0:T(8,128)(2,1)S(1)} collective-permute-done((bf16[128,512]{1,0:T(8,128)(2,1)S(1)}, bf16[128,512]{1,0:T(8,128)(2,1)S(1)}, u32[]{:S(2)}, u32[]{:S(2)}) %collective-permute-start.6) | collective-permute-done | bytes 131104 | tf_op jit(solution)/shard_map/ppermute | solution.py:26
  29.2 0.0 collective-permute-done.7.c
  29.2 0.7 %shard_map.90 = bf16[128,512]{1,0:T(8,128)(2,1)} custom-call(f32[128,512]{1,0:T(8,128)S(1)} %get-tuple-element.33.a, bf16[128,512]{1,0:T(8,128)(2,1)S(1)} %collective-permute-done.6.b, bf16[128,512]{1,0:T(8,128)(2,1)S(1)} %collective-permute-done.7.c), custom_call_target="tpu_custom_call" | custom-call | bytes 1048576 | tf_op jit(solution)/shard_map/pallas_call | solution.py:192
Async XLA Ops:
  0.6 7.4 %copy-start = (s32[256,3,2,2]{0,3,2,1:T(2,128)S(1)}, s32[256,3,2,2]{0,3,2,1:T(2,128)}, u32[]{:S(2)}) copy-start(s32[256,3,2,2]{0,3,2,1:T(2,128)} %param.11) | copy-start | bytes 36868
  0.6 13.1 %collective-permute-start.3 = (bf16[128,512]{1,0:T(8,128)(2,1)}, bf16[128,512]{1,0:T(8,128)(2,1)S(1)}, u32[]{:S(2)}, u32[]{:S(2)}) collective-permute-start(bf16[128,512]{1,0:T(8,128)(2,1)} %keys.1), channel_id=1, source_target_pairs={{252,0},{0,4},{4,8},{8,12},{12,16},{16,20},{20,24},{24,28},{28,32}... | collective-permute-start | bytes 393224 | tf_op jit(solution)/shard_map/ppermute | solution.py:26
  2.8 11.0 %collective-permute-start.2 = (bf16[128,512]{1,0:T(8,128)(2,1)}, bf16[128,512]{1,0:T(8,128)(2,1)S(1)}, u32[]{:S(2)}, u32[]{:S(2)}) collective-permute-start(bf16[128,512]{1,0:T(8,128)(2,1)} %keys.1), channel_id=1, source_target_pairs={{3,0},{0,1},{1,2},{2,3},{7,4},{4,5},{5,6},{6,7},{11,8},{8,9},{9,10... | collective-permute-start | bytes 393224 | tf_op jit(solution)/shard_map/ppermute | solution.py:26
  6.5 13.4 %collective-permute-start.1 = (bf16[128,512]{1,0:T(8,128)(2,1)}, bf16[128,512]{1,0:T(8,128)(2,1)S(1)}, u32[]{:S(2)}, u32[]{:S(2)}) collective-permute-start(bf16[128,512]{1,0:T(8,128)(2,1)} %values.1), channel_id=1, source_target_pairs={{252,0},{0,4},{4,8},{8,12},{12,16},{16,20},{20,24},{24,28},{28,32}... | collective-permute-start | bytes 393224 | tf_op jit(solution)/shard_map/ppermute | solution.py:26
  7.7 12.2 %collective-permute-start = (bf16[128,512]{1,0:T(8,128)(2,1)}, bf16[128,512]{1,0:T(8,128)(2,1)S(1)}, u32[]{:S(2)}, u32[]{:S(2)}) collective-permute-start(bf16[128,512]{1,0:T(8,128)(2,1)} %values.1), channel_id=1, source_target_pairs={{3,0},{0,1},{1,2},{2,3},{7,4},{4,5},{5,6},{6,7},{11,8},{8,9},{9,10... | collective-permute-start | bytes 393224 | tf_op jit(solution)/shard_map/ppermute | solution.py:26
  16.4 9.4 %collective-permute-start.4 = (bf16[128,512]{1,0:T(8,128)(2,1)S(1)}, bf16[128,512]{1,0:T(8,128)(2,1)S(1)}, u32[]{:S(2)}, u32[]{:S(2)}) collective-permute-start(bf16[128,512]{1,0:T(8,128)(2,1)S(1)} %get-tuple-element.28), channel_id=1, source_target_pairs={{1,0},{2,1},{3,2},{0,3},{5,4},{6,5},{7,6},{4,7},{9,8},{10,9},{11,1... | collective-permute-start | bytes 393224 | tf_op jit(solution)/shard_map/ppermute | solution.py:26
  17.7 8.0 %collective-permute-start.5 = (bf16[128,512]{1,0:T(8,128)(2,1)S(1)}, bf16[128,512]{1,0:T(8,128)(2,1)S(1)}, u32[]{:S(2)}, u32[]{:S(2)}) collective-permute-start(bf16[128,512]{1,0:T(8,128)(2,1)S(1)} %get-tuple-element.29), channel_id=1, source_target_pairs={{4,0},{8,4},{12,8},{16,12},{20,16},{24,20},{28,24},{32,28},{36,32}... | collective-permute-start | bytes 393224 | tf_op jit(solution)/shard_map/ppermute | solution.py:26
  22.7 6.5 %collective-permute-start.6 = (bf16[128,512]{1,0:T(8,128)(2,1)S(1)}, bf16[128,512]{1,0:T(8,128)(2,1)S(1)}, u32[]{:S(2)}, u32[]{:S(2)}) collective-permute-start(bf16[128,512]{1,0:T(8,128)(2,1)S(1)} %get-tuple-element.34), channel_id=1, source_target_pairs={{1,0},{2,1},{3,2},{0,3},{5,4},{6,5},{7,6},{4,7},{9,8},{10,9},{11,1... | collective-permute-start | bytes 393224 | tf_op jit(solution)/shard_map/ppermute | solution.py:26
  24.1 5.2 %collective-permute-start.7 = (bf16[128,512]{1,0:T(8,128)(2,1)S(1)}, bf16[128,512]{1,0:T(8,128)(2,1)S(1)}, u32[]{:S(2)}, u32[]{:S(2)}) collective-permute-start(bf16[128,512]{1,0:T(8,128)(2,1)S(1)} %get-tuple-element.35), channel_id=1, source_target_pairs={{4,0},{8,4},{12,8},{16,12},{20,16},{24,20},{28,24},{32,28},{36,32}... | collective-permute-start | bytes 393224 | tf_op jit(solution)/shard_map/ppermute | solution.py:26

commit v3 on v2

v3 whole, which is shorter than its diff:
```python
import functools

import jax
import jax.numpy as jnp
from jax import lax
from jax.experimental import pallas as pl
from jax.experimental.pallas import tpu as pltpu
from jax.sharding import PartitionSpec as P

HEAD_DIM = 128
SCALE = HEAD_DIM ** -0.5
LOG2E = 1.4426950408889634
NEG_BIG = -1e30
VMEM = 16 * 1024 * 1024
NT = (((1,), (1,)), ((), ()))
NN = (((1,), (0,)), ((), ()))
TN = (((0,), (0,)), ((), ()))


def dot(a, b, dims):
    return lax.dot_general(a, b, dims, preferred_element_type=jnp.float32)


def ring(block, axis, step):
    size = lax.axis_size(axis)
    return lax.ppermute(block, axis, [(i, (i + step) % size) for i in range(size)])


def head(ref, h, count=1):
    return ref[:, h * HEAD_DIM : (h + count) * HEAD_DIM]


def stack_heads(ref, first, count):
    return jnp.concatenate([head(ref, first + e) for e in range(count)], axis=0)


def stack_sources(refs, h):
    return jnp.concatenate([head(ref, h) for ref in refs], axis=0)


def fill_bias(holder, inner_prev, outer_prev, order, keep, bias):
    stretch = bias.shape[1] // 2
    lane = lax.broadcasted_iota(jnp.int32, (stretch, 2 * stretch), 1)
    line = lax.broadcasted_iota(jnp.int32, (stretch, 2 * stretch), 0)
    place = lax.broadcasted_iota(jnp.int32, order.shape, 1)
    first = lane < stretch

    def pick(table, column):
        return jnp.sum(jnp.where(place == column, table, 0), axis=1, keepdims=True)

    numbers = [pick(order[...], column) for column in (holder, inner_prev, outer_prev)]
    own = numbers[0]
    query_pos = jnp.where(first, own[0:1] * stretch + lane, (own[1:2] - 1) * stretch + lane)
    for s in range(3):
        flags = [pick(keep[s, a], holder) for a in range(2)]
        for b in range(2):
            flag = jnp.where(first, flags[0][b : b + 1], flags[1][b : b + 1])
            if s == 0:
                flag = jnp.where(first if b == 0 else ~first, 1, flag)
            key_pos = numbers[s][b : b + 1] * stretch + line
            allowed = (flag > 0) & (key_pos <= query_pos)
            row = (2 * s + b) * stretch
            bias[row : row + stretch, :] = jnp.where(allowed, 0.0, NEG_BIG)


def stage_kernel(orders, keeps, queries, grads, keys, values, q, g, k, v, bias, order, keep, sems):
    moves = ((orders, order), (keeps, keep), (values, v), (keys, k), (queries, q), (grads, g))
    copies = [pltpu.make_async_copy(*move, sems.at[n]) for n, move in enumerate(moves)]
    for copy in copies:
        copy.start()
    for copy in copies[:2]:
        copy.wait()
    n_inner, n_outer = lax.axis_size("inner"), lax.axis_size("outer")
    pos_inner, pos_outer = lax.axis_index("inner"), lax.axis_index("outer")
    inner_prev = lax.rem(pos_inner + n_inner - 1, n_inner)
    outer_prev = lax.rem(pos_outer + n_outer - 1, n_outer)
    fill_bias(
        pos_outer * n_inner + pos_inner,
        pos_outer * n_inner + inner_prev,
        outer_prev * n_inner + pos_inner,
        order,
        keep,
        bias,
    )
    for copy in copies[2:]:
        copy.wait()


def pairs(group, kv_heads):
    for h in range(kv_heads):
        for pair in range(group // 2):
            yield h, h * group + 2 * pair, slice(2 * pair * HEAD_DIM, (2 * pair + 2) * HEAD_DIM)


def masked_scores(keys, query, bias):
    return dot(keys, query, NT) * (SCALE * LOG2E) + jnp.concatenate([bias, bias], axis=1)


def own_kernel(group, bias, q, g, k, v, raised, grad_probs, stats):
    span = q.shape[0]
    for h, first, cols in pairs(group, k.shape[1] // HEAD_DIM):
        scores = masked_scores(head(k, h), stack_heads(q, first, 2), bias[:span])
        peak = jnp.max(scores, axis=0, keepdims=True)
        weight = jnp.exp2(scores - peak)
        grads = dot(head(v, h), stack_heads(g, first, 2), NT)
        raised[h, :, cols] = weight.astype(jnp.bfloat16)
        grad_probs[h, :, cols] = grads
        stats[h, 0:1, cols] = peak
        stats[h, 1:2, cols] = jnp.sum(weight, axis=0, keepdims=True)
        stats[h, 2:3, cols] = jnp.sum(weight * grads, axis=0, keepdims=True)


def write_terms(outs, outer, inner):
    span = inner.shape[0]
    for h, out in enumerate(outs):
        lanes = slice(h * HEAD_DIM, (h + 1) * HEAD_DIM)
        inner[:, lanes] = out[:span].astype(inner.dtype)
        outer[:, lanes] = out[span:].astype(outer.dtype)


def probs_kernel(group, bias, q, g, ki, ko, stats, probs, rows, outer, inner, work):
    span = q.shape[0]
    outs = []
    for h, first, cols in pairs(group, ki.shape[1] // HEAD_DIM):
        if first == h * group:
            keys = stack_sources((ki, ko), h)
        scores = masked_scores(keys, stack_heads(q, first, 2), bias[span:])
        own_peak = stats[h, 0:1, cols]
        peak = jnp.maximum(own_peak, jnp.max(scores, axis=0, keepdims=True))
        raised = jnp.exp2(scores - peak)
        lowered = jnp.exp2(own_peak - peak)
        scale = 1.0 / (jnp.sum(raised, axis=0, keepdims=True) + lowered * stats[h, 1:2, cols])
        work[h, :, cols] = (raised * scale).astype(jnp.bfloat16)
        rows[h, 0:1, cols] = lowered * scale
        rows[h, 1:2, cols] = lowered * scale * stats[h, 2:3, cols]
        if first == (h + 1) * group - 2:
            outs.append(dot(work[h], stack_heads(g, h * group, group), NN))
    write_terms(outs, outer, inner)
    probs[...] = work[...]


def scores_kernel(group, q, g, vi, vo, probs, rows, dscores, deltas, outer, inner, work):
    outs = []
    for h, first, cols in pairs(group, vi.shape[1] // HEAD_DIM):
        if first == h * group:
            values = stack_sources((vi, vo), h)
        grad_probs = dot(values, stack_heads(g, first, 2), NT)
        weight = probs[h, :, cols].astype(jnp.float32)
        delta = rows[h, 1:2, cols] + jnp.sum(weight * grad_probs, axis=0, keepdims=True)
        work[h, :, cols] = (weight * (grad_probs - delta)).astype(jnp.bfloat16)
        deltas[h, 0:1, cols] = delta
        if first == (h + 1) * group - 2:
            outs.append(dot(work[h], stack_heads(q, h * group, group), NN) * SCALE)
    write_terms(outs, outer, inner)
    dscores[...] = work[...]


def queries_kernel(
    group, q, g, ks, ki, ko, raised, grad_probs, rows, deltas, dscores, dvi, dvo, dq, dk, dv, own_probs, own_scores
):
    f32, bf16 = jnp.float32, jnp.bfloat16
    kv_heads = ks.shape[1] // HEAD_DIM
    for h, first, cols in pairs(group, kv_heads):
        weight = raised[h, :, cols].astype(f32) * rows[h, 0:1, cols]
        own_probs[h, :, cols] = weight.astype(bf16)
        own_scores[h, :, cols] = (weight * (grad_probs[h, :, cols] - deltas[h, 0:1, cols])).astype(bf16)
    outs = []
    for h in range(kv_heads):
        lanes = slice(h * HEAD_DIM, (h + 1) * HEAD_DIM)
        terms = dvi[:, lanes].astype(f32) + dvo[:, lanes].astype(f32)
        dv[:, lanes] = (dot(own_probs[h], stack_heads(g, h * group, group), NN) + terms).astype(bf16)
        dk[:, lanes] = dot(own_scores[h], stack_heads(q, h * group, group), NN) * SCALE
        wide = jnp.concatenate([own_scores[h], dscores[h]], axis=0)
        outs.append((dot(stack_sources((ks, ki, ko), h), wide, TN) * SCALE).astype(bf16))
    for h, out in enumerate(outs):
        for e in range(group):
            lanes = slice((h * group + e) * HEAD_DIM, (h * group + e + 1) * HEAD_DIM)
            dq[:, lanes] = out[:, e * HEAD_DIM : (e + 1) * HEAD_DIM].T


def gate_kernel(x, vi, vo, out):
    out[...] = x[...]


def add_kernel(a, b, c, out):
    out[...] = (a[...] + b[...].astype(jnp.float32) + c[...].astype(jnp.float32)).astype(out.dtype)


def shards(queries, keys, values, grad_out, stretch_order, block_keep):
    span = keys.shape[0]
    width = keys.shape[1]
    kv_heads = width // HEAD_DIM
    group = queries.shape[1] // width

    f32, bf16 = jnp.float32, jnp.bfloat16
    vmem = pl.BlockSpec(memory_space=pltpu.VMEM)
    hbm = pl.BlockSpec(memory_space=pltpu.HBM)
    rows = jax.ShapeDtypeStruct(queries.shape, bf16)
    wide = group * HEAD_DIM
    away = jax.ShapeDtypeStruct((kv_heads, 2 * span, wide), bf16)
    own16 = jax.ShapeDtypeStruct((kv_heads, span, wide), bf16)
    own32 = jax.ShapeDtypeStruct((kv_heads, span, wide), f32)
    stat = jax.ShapeDtypeStruct((kv_heads, 8, wide), f32)
    kv32 = jax.ShapeDtypeStruct((span, width), f32)
    kv16 = jax.ShapeDtypeStruct((span, width), bf16)
    work = [pltpu.VMEM(away.shape, bf16)]

    def call(kernel, ins, out_shape, scratch=()):
        return pl.pallas_call(
            kernel,
            in_specs=ins,
            out_specs=[vmem] * len(out_shape),
            out_shape=out_shape,
            scratch_shapes=scratch,
            compiler_params=pltpu.CompilerParams(vmem_limit_bytes=VMEM),
            cost_estimate=pl.CostEstimate(flops=1, bytes_accessed=1, transcendentals=0),
        )

    def run(kernel, ins, out_shape, scratch=()):
        return call(functools.partial(kernel, group), [vmem] * len(ins), out_shape, scratch)(*ins)

    k_out = ring(keys, "outer", 1)
    k_in = ring(keys, "inner", 1)
    tables = stretch_order.T, block_keep.transpose(1, 2, 3, 0)
    q, g, k, v, bias = call(
        stage_kernel,
        [hbm] * 6,
        [rows, rows, kv16, kv16, jax.ShapeDtypeStruct((3 * span, span), f32)],
        [pltpu.VMEM(x.shape, x.dtype) for x in tables] + [pltpu.SemaphoreType.DMA((6,))],
    )(*(pltpu.with_memory_space_constraint(x, pltpu.HBM) for x in (*tables, queries, grad_out, keys, values)))
    v_out = ring(v, "outer", 1)
    v_in = ring(v, "inner", 1)
    raised, grad_probs, stats = run(own_kernel, (bias, q, g, k, v), [own16, own32, stat])
    probs, row_scale, dvo, dvi = run(
        probs_kernel, (bias, q, g, k_in, k_out, stats), [away, stat, kv16, kv16], work
    )
    dv_in = ring(dvi, "inner", -1)
    (dvo,) = call(gate_kernel, [vmem] * 3, [kv16])(dvo, v_in, v_out)
    dv_out = ring(dvo, "outer", -1)
    dscores, deltas, dko, dki = run(
        scores_kernel, (q, g, v_in, v_out, probs, row_scale), [away, stat, kv16, kv16], work
    )
    dk_in = ring(dki, "inner", -1)
    dk_out = ring(dko, "outer", -1)
    dq, dks, dv = run(
        queries_kernel,
        (q, g, k, k_in, k_out, raised, grad_probs, row_scale, deltas, dscores, dv_in, dv_out),
        [rows, kv32, kv16],
        [pltpu.VMEM(own16.shape, bf16)] * 2,
    )
    (dk,) = call(add_kernel, [vmem] * 3, [kv16])(dks, dk_in, dk_out)
    return dq, dk, dv


def solution(mesh):
    rows = P(("outer", "inner"), None)
    return jax.shard_map(
        shards, mesh=mesh, in_specs=(rows, rows, rows, rows, P(), P()), out_specs=(rows, rows, rows), check_vma=False
    )
```

time: 30.1 us -> 28.8 us (0.957)
  local copies, waits for them, and re-layouts: 1.33 us -> 0 us
  waiting for transfers between devices: 3.81 us -> 4.69 us
  starting transfers between devices: 13.9 us -> 13.1 us
    dynamic_slice x2 -> x0, local copies, waits for them, and re-layouts: 1.23 us -> none  [the longest x1 0.98 us: shards(): lax.dynamic_index_in_dim(stretch_order, h, 0, False)]
    ppermute x8, waiting for transfers between devices: 3.81 us -> 4.69 us  [ring(): lax.ppermute(block, axis, [(i, (i + step) % size) for i in range(size)])]
    ppermute x8, starting transfers between devices: 13.9 us -> 13.1 us  [ring(): lax.ppermute(block, axis, [(i, (i + step) % size) for i in range(size)])]
    pallas_call x6 -> x7, Pallas kernels: 10.2 us -> 10.2 us  [the longest x4 7.77 us: run(): call(functools.partial(kernel, group), [vmem] * len(ins), out_shape, scra...]
  transfers between devices with their start and end apart: 8 -> 8, of which waited for: 2 -> 3; matrix products, arithmetic and copies ran while one was open for 5% -> 0% of each run, Pallas kernels for 32% -> 33%
where the time goes in v3:
time: 28.8 us; the launch traced here: 28.7 us
  starting transfers between devices  13.1 us (45%)
  Pallas kernels  10.2 us (35%)
  waiting for transfers between devices  4.69 us (16%)
  between operations  0.67 us (2%)
    ppermute x8, starting transfers between devices, ring(): lax.ppermute(block, axis, [(i, (i + step) % size) for i in range(size)])  13.1 us
    pallas_call x4, Pallas kernels, run(): call(functools.partial(kernel, group), [vmem] * len(ins), out_shape, scra...  7.77 us
    ppermute x8, waiting for transfers between devices, ring(): lax.ppermute(block, axis, [(i, (i + step) % size) for i in range(size)])  4.69 us
    pallas_call x1, Pallas kernels, shards(): call(stage_kernel, [hbm] * 6, [rows, rows, kv16, kv16, jax.ShapeDtypeStru...  1.76 us
    pallas_call x1, Pallas kernels, shards(): dk, = call(add_kernel, [vmem] * 3, [kv16])(dks, dk_in, dk_out)  0.7 us
  transfers between devices with their start and end apart: 8, of which 3 were waited for; matrix products, arithmetic and copies ran while one was open for 0% of the time, Pallas kernels for 33%

profile of v3, /device:TPU:1, one launch (start us, length us, event | category | flops | bytes accessed | tf_op | source)
XLA Modules:
  0.0 28.7 jit_solution(621317986026026607)
XLA Ops:
  0.6 2.1 %collective-permute-start.1 = (bf16[128,512]{1,0:T(8,128)(2,1)}, bf16[128,512]{1,0:T(8,128)(2,1)S(1)}, u32[]{:S(2)}, u32[]{:S(2)}) collective-permute-start(bf16[128,512]{1,0:T(8,128)(2,1)} %keys.1), channel_id=1, source_target_pairs={{0,4},{4,8},{8,12},{12,16},{16,20},{20,24},{24,28},{28,32},{32,36}... | collective-permute-start | bytes 393224 | tf_op jit(solution)/shard_map/ppermute | solution.py:26
  2.8 3.8 %collective-permute-start = (bf16[128,512]{1,0:T(8,128)(2,1)}, bf16[128,512]{1,0:T(8,128)(2,1)S(1)}, u32[]{:S(2)}, u32[]{:S(2)}) collective-permute-start(bf16[128,512]{1,0:T(8,128)(2,1)} %keys.1), channel_id=1, source_target_pairs={{0,1},{1,2},{2,3},{3,0},{4,5},{5,6},{6,7},{7,4},{8,9},{9,10},{10,1... | collective-permute-start | bytes 393224 | tf_op jit(solution)/shard_map/ppermute | solution.py:26
  6.5 1.8 %shard_map.85 = (bf16[128,4096]{1,0:T(8,128)(2,1)S(1)}, bf16[128,4096]{1,0:T(8,128)(2,1)S(1)}, bf16[128,512]{1,0:T(8,128)(2,1)S(1)}, bf16[128,512]{1,0:T(8,128)(2,1)S(1)}, f32[384,128]{1,0:T(8,128)S(1)}) custom-call(s32[2,256]{1,0:T(2,128)} %bitcast.3, s32[3,2,2,256]{3,2,1,0:T(2,128)} %bitcast.2, bf16[128,4096]{1,0:T(8,128)(2,1)} %queries.1, ...), custom_call_target="tpu_custom_call" | custom-call | flops 1 | bytes 1 | tf_op jit(solution)/shard_map/pallas_call | solution.py:225
  8.3 1.3 %collective-permute-start.3 = (bf16[128,512]{1,0:T(8,128)(2,1)S(1)}, bf16[128,512]{1,0:T(8,128)(2,1)S(1)}, u32[]{:S(2)}, u32[]{:S(2)}) collective-permute-start(bf16[128,512]{1,0:T(8,128)(2,1)S(1)} %get-tuple-element.26.v), channel_id=1, source_target_pairs={{0,4},{4,8},{8,12},{12,16},{16,20},{20,24},{24,28},{28,32},{32,36}... | collective-permute-start | bytes 393224 | tf_op jit(solution)/shard_map/ppermute | solution.py:26
  9.6 0.3 collective-permute-start.2
  9.8 1.0 %shard_map.86 = (bf16[4,128,1024]{2,1,0:T(8,128)(2,1)S(1)}, f32[4,128,1024]{2,1,0:T(8,128)S(1)}, f32[4,8,1024]{2,1,0:T(8,128)S(1)}) custom-call(f32[384,128]{1,0:T(8,128)S(1)} %get-tuple-element.25.bias, bf16[128,4096]{1,0:T(8,128)(2,1)S(1)} %get-tuple-element.22.q, bf16[128,4096]{1,0:T(8,128)(2,1)S(1)} %get-tuple-element.23.g, ...), custom_call_target="tpu_custom_call" | custom-call | flops 1 | bytes 1 | tf_op jit(solution)/shard_map/pallas_call | solution.py:220
  10.9 2.9 %collective-permute-done.1.ko = bf16[128,512]{1,0:T(8,128)(2,1)S(1)} collective-permute-done((bf16[128,512]{1,0:T(8,128)(2,1)}, bf16[128,512]{1,0:T(8,128)(2,1)S(1)}, u32[]{:S(2)}, u32[]{:S(2)}) %collective-permute-start.1) | collective-permute-done | bytes 131104 | tf_op jit(solution)/shard_map/ppermute | solution.py:26
  13.8 0.0 collective-permute-done.ki
  13.8 2.2 %shard_map.87 = (bf16[4,256,1024]{2,1,0:T(8,128)(2,1)S(1)}, f32[4,8,1024]{2,1,0:T(8,128)S(1)}, bf16[128,512]{1,0:T(8,128)(2,1)S(1)}, bf16[128,512]{1,0:T(8,128)(2,1)S(1)}) custom-call(f32[384,128]{1,0:T(8,128)S(1)} %get-tuple-element.25.bias, bf16[128,4096]{1,0:T(8,128)(2,1)S(1)} %get-tuple-element.22.q, bf16[128,4096]{1,0:T(8,128)(2,1)S(1)} %get-tuple-element.23.g, ...), custom_call_target="tpu_custom_call" | custom-call | flops 1 | bytes 1 | tf_op jit(solution)/shard_map/pallas_call | solution.py:220
  16.0 1.2 %collective-permute-done.3.vo = bf16[128,512]{1,0:T(8,128)(2,1)S(1)} collective-permute-done((bf16[128,512]{1,0:T(8,128)(2,1)S(1)}, bf16[128,512]{1,0:T(8,128)(2,1)S(1)}, u32[]{:S(2)}, u32[]{:S(2)}) %collective-permute-start.3) | collective-permute-done | bytes 131104 | tf_op jit(solution)/shard_map/ppermute | solution.py:26
  17.2 0.0 collective-permute-done.2.vi
  17.2 1.7 %collective-permute-start.5 = (bf16[128,512]{1,0:T(8,128)(2,1)S(1)}, bf16[128,512]{1,0:T(8,128)(2,1)S(1)}, u32[]{:S(2)}, u32[]{:S(2)}) collective-permute-start(bf16[128,512]{1,0:T(8,128)(2,1)S(1)} %shard_map.89), channel_id=1, source_target_pairs={{0,252},{4,0},{8,4},{12,8},{16,12},{20,16},{24,20},{28,24},{32,28}... | collective-permute-start | bytes 393224 | tf_op jit(solution)/shard_map/ppermute | solution.py:26
  18.9 0.9 %collective-permute-start.4 = (bf16[128,512]{1,0:T(8,128)(2,1)S(1)}, bf16[128,512]{1,0:T(8,128)(2,1)S(1)}, u32[]{:S(2)}, u32[]{:S(2)}) collective-permute-start(bf16[128,512]{1,0:T(8,128)(2,1)S(1)} %get-tuple-element.34), channel_id=1, source_target_pairs={{0,3},{1,0},{2,1},{3,2},{4,7},{5,4},{6,5},{7,6},{8,11},{9,8},{10,9... | collective-permute-start | bytes 393224 | tf_op jit(solution)/shard_map/ppermute | solution.py:26
  19.8 2.2 %shard_map.88 = (bf16[4,256,1024]{2,1,0:T(8,128)(2,1)S(1)}, f32[4,8,1024]{2,1,0:T(8,128)S(1)}, bf16[128,512]{1,0:T(8,128)(2,1)S(1)}, bf16[128,512]{1,0:T(8,128)(2,1)S(1)}) custom-call(bf16[128,4096]{1,0:T(8,128)(2,1)S(1)} %get-tuple-element.22.q, bf16[128,4096]{1,0:T(8,128)(2,1)S(1)} %get-tuple-element.23.g, bf16[128,512]{1,0:T(8,128)(2,1)S(1)} %collective-permute-done.2.vi, ...), custom_call_target="tpu_custom_call" | custom-call | flops 1 | bytes 1 | tf_op jit(solution)/shard_map/pallas_call | solution.py:220
  22.0 2.0 %collective-permute-start.6 = (bf16[128,512]{1,0:T(8,128)(2,1)S(1)}, bf16[128,512]{1,0:T(8,128)(2,1)S(1)}, u32[]{:S(2)}, u32[]{:S(2)}) collective-permute-start(bf16[128,512]{1,0:T(8,128)(2,1)S(1)} %get-tuple-element.38), channel_id=1, source_target_pairs={{0,3},{1,0},{2,1},{3,2},{4,7},{5,4},{6,5},{7,6},{8,11},{9,8},{10,9... | collective-permute-start | bytes 393224 | tf_op jit(solution)/shard_map/ppermute | solution.py:26
  24.0 1.0 %collective-permute-start.7 = (bf16[128,512]{1,0:T(8,128)(2,1)S(1)}, bf16[128,512]{1,0:T(8,128)(2,1)S(1)}, u32[]{:S(2)}, u32[]{:S(2)}) collective-permute-start(bf16[128,512]{1,0:T(8,128)(2,1)S(1)} %get-tuple-element.39), channel_id=1, source_target_pairs={{0,252},{4,0},{8,4},{12,8},{16,12},{20,16},{24,20},{28,24},{32,28}... | collective-permute-start | bytes 393224 | tf_op jit(solution)/shard_map/ppermute | solution.py:26
  25.0 0.0 collective-permute-done.5.dvo
  25.0 0.0 collective-permute-done.4.dvi
  25.0 2.4 %shard_map.90 = (bf16[128,4096]{1,0:T(8,128)(2,1)}, f32[128,512]{1,0:T(8,128)S(1)}, bf16[128,512]{1,0:T(8,128)(2,1)}) custom-call(bf16[128,4096]{1,0:T(8,128)(2,1)S(1)} %get-tuple-element.22.q, bf16[128,4096]{1,0:T(8,128)(2,1)S(1)} %get-tuple-element.23.g, bf16[128,512]{1,0:T(8,128)(2,1)S(1)} %get-tuple-element.24.k.ks, ...), custom_call_target="tpu_custom_call" | custom-call | flops 1 | bytes 1 | tf_op jit(solution)/shard_map/pallas_call | solution.py:220
  27.4 0.6 %collective-permute-done.6.b = bf16[128,512]{1,0:T(8,128)(2,1)S(1)} collective-permute-done((bf16[128,512]{1,0:T(8,128)(2,1)S(1)}, bf16[128,512]{1,0:T(8,128)(2,1)S(1)}, u32[]{:S(2)}, u32[]{:S(2)}) %collective-permute-start.6) | collective-permute-done | bytes 131104 | tf_op jit(solution)/shard_map/ppermute | solution.py:26
  28.0 0.0 collective-permute-done.7.c
  28.0 0.7 %shard_map.91 = bf16[128,512]{1,0:T(8,128)(2,1)} custom-call(f32[128,512]{1,0:T(8,128)S(1)} %get-tuple-element.37.a, bf16[128,512]{1,0:T(8,128)(2,1)S(1)} %collective-permute-done.6.b, bf16[128,512]{1,0:T(8,128)(2,1)S(1)} %collective-permute-done.7.c), custom_call_target="tpu_custom_call" | custom-call | flops 1 | bytes 1 | tf_op jit(solution)/shard_map/pallas_call | solution.py:251
  (1 shorter events, 0.0 us)
Async XLA Ops:
  0.6 13.1 %collective-permute-start.1 = (bf16[128,512]{1,0:T(8,128)(2,1)}, bf16[128,512]{1,0:T(8,128)(2,1)S(1)}, u32[]{:S(2)}, u32[]{:S(2)}) collective-permute-start(bf16[128,512]{1,0:T(8,128)(2,1)} %keys.1), channel_id=1, source_target_pairs={{0,4},{4,8},{8,12},{12,16},{16,20},{20,24},{24,28},{28,32},{32,36}... | collective-permute-start | bytes 393224 | tf_op jit(solution)/shard_map/ppermute | solution.py:26
  2.8 11.0 %collective-permute-start = (bf16[128,512]{1,0:T(8,128)(2,1)}, bf16[128,512]{1,0:T(8,128)(2,1)S(1)}, u32[]{:S(2)}, u32[]{:S(2)}) collective-permute-start(bf16[128,512]{1,0:T(8,128)(2,1)} %keys.1), channel_id=1, source_target_pairs={{0,1},{1,2},{2,3},{3,0},{4,5},{5,6},{6,7},{7,4},{8,9},{9,10},{10,1... | collective-permute-start | bytes 393224 | tf_op jit(solution)/shard_map/ppermute | solution.py:26
  8.3 8.9 %collective-permute-start.3 = (bf16[128,512]{1,0:T(8,128)(2,1)S(1)}, bf16[128,512]{1,0:T(8,128)(2,1)S(1)}, u32[]{:S(2)}, u32[]{:S(2)}) collective-permute-start(bf16[128,512]{1,0:T(8,128)(2,1)S(1)} %get-tuple-element.26.v), channel_id=1, source_target_pairs={{0,4},{4,8},{8,12},{12,16},{16,20},{20,24},{24,28},{28,32},{32,36}... | collective-permute-start | bytes 393224 | tf_op jit(solution)/shard_map/ppermute | solution.py:26
  9.6 7.6 %collective-permute-start.2 = (bf16[128,512]{1,0:T(8,128)(2,1)S(1)}, bf16[128,512]{1,0:T(8,128)(2,1)S(1)}, u32[]{:S(2)}, u32[]{:S(2)}) collective-permute-start(bf16[128,512]{1,0:T(8,128)(2,1)S(1)} %get-tuple-element.26.v), channel_id=1, source_target_pairs={{0,1},{1,2},{2,3},{3,0},{4,5},{5,6},{6,7},{7,4},{8,9},{9,10},{10,1... | collective-permute-start | bytes 393224 | tf_op jit(solution)/shard_map/ppermute | solution.py:26
  17.2 7.8 %collective-permute-start.5 = (bf16[128,512]{1,0:T(8,128)(2,1)S(1)}, bf16[128,512]{1,0:T(8,128)(2,1)S(1)}, u32[]{:S(2)}, u32[]{:S(2)}) collective-permute-start(bf16[128,512]{1,0:T(8,128)(2,1)S(1)} %shard_map.89), channel_id=1, source_target_pairs={{0,252},{4,0},{8,4},{12,8},{16,12},{20,16},{24,20},{28,24},{32,28}... | collective-permute-start | bytes 393224 | tf_op jit(solution)/shard_map/ppermute | solution.py:26
  18.9 6.1 %collective-permute-start.4 = (bf16[128,512]{1,0:T(8,128)(2,1)S(1)}, bf16[128,512]{1,0:T(8,128)(2,1)S(1)}, u32[]{:S(2)}, u32[]{:S(2)}) collective-permute-start(bf16[128,512]{1,0:T(8,128)(2,1)S(1)} %get-tuple-element.34), channel_id=1, source_target_pairs={{0,3},{1,0},{2,1},{3,2},{4,7},{5,4},{6,5},{7,6},{8,11},{9,8},{10,9... | collective-permute-start | bytes 393224 | tf_op jit(solution)/shard_map/ppermute | solution.py:26
  22.0 6.0 %collective-permute-start.6 = (bf16[128,512]{1,0:T(8,128)(2,1)S(1)}, bf16[128,512]{1,0:T(8,128)(2,1)S(1)}, u32[]{:S(2)}, u32[]{:S(2)}) collective-permute-start(bf16[128,512]{1,0:T(8,128)(2,1)S(1)} %get-tuple-element.38), channel_id=1, source_target_pairs={{0,3},{1,0},{2,1},{3,2},{4,7},{5,4},{6,5},{7,6},{8,11},{9,8},{10,9... | collective-permute-start | bytes 393224 | tf_op jit(solution)/shard_map/ppermute | solution.py:26
  24.0 4.0 %collective-permute-start.7 = (bf16[128,512]{1,0:T(8,128)(2,1)S(1)}, bf16[128,512]{1,0:T(8,128)(2,1)S(1)}, u32[]{:S(2)}, u32[]{:S(2)}) collective-permute-start(bf16[128,512]{1,0:T(8,128)(2,1)S(1)} %get-tuple-element.39), channel_id=1, source_target_pairs={{0,252},{4,0},{8,4},{12,8},{16,12},{20,16},{24,20},{28,24},{32,28}... | collective-permute-start | bytes 393224 | tf_op jit(solution)/shard_map/ppermute | solution.py:26

commit v4 on v3

--- a/solution.py
+++ b/solution.py
@@ -118,45 +118,96 @@
         outer[:, lanes] = out[span:].astype(outer.dtype)
 
 
-def probs_kernel(group, bias, q, g, ki, ko, stats, probs, rows, outer, inner, work):
+def by_pairs(group, kv_heads, product, finish, gather):
+    steps = list(pairs(group, kv_heads))
+    outs = []
+    ahead = product(*steps[0])
+    for n, step in enumerate(steps):
+        block = ahead
+        if n + 1 < len(steps):
+            ahead = product(*steps[n + 1])
+        h, first, cols = step
+        if gather and h > 0 and first == h * group + 2:
+            outs.append(gather(h - 1))
+        finish(h, cols, block)
+    if gather:
+        outs.append(gather(kv_heads - 1))
+    return outs
+
+
+def outer_kernel(group, bias, q, ko, raised, stats, work, rows):
     span = q.shape[0]
-    outs = []
-    for h, first, cols in pairs(group, ki.shape[1] // HEAD_DIM):
-        if first == h * group:
-            keys = stack_sources((ki, ko), h)
-        scores = masked_scores(keys, stack_heads(q, first, 2), bias[span:])
-        own_peak = stats[h, 0:1, cols]
-        peak = jnp.maximum(own_peak, jnp.max(scores, axis=0, keepdims=True))
-        raised = jnp.exp2(scores - peak)
-        lowered = jnp.exp2(own_peak - peak)
-        scale = 1.0 / (jnp.sum(raised, axis=0, keepdims=True) + lowered * stats[h, 1:2, cols])
-        work[h, :, cols] = (raised * scale).astype(jnp.bfloat16)
+
+    def finish(h, cols, products):
+        scores = products * (SCALE * LOG2E) + jnp.concatenate([bias[2 * span :]] * 2, axis=1)
+        peak = jnp.max(scores, axis=0, keepdims=True)
+        weight = jnp.exp2(scores - peak)
+        work[h, :, cols] = weight.astype(jnp.bfloat16)
+        rows[h, 0:1, cols] = peak
+        rows[h, 1:2, cols] = jnp.sum(weight, axis=0, keepdims=True)
+
+    by_pairs(
+        group,
+        ko.shape[1] // HEAD_DIM,
+        lambda h, first, cols: dot(head(ko, h), stack_heads(q, first, 2), NT),
+        finish,
+        None,
+    )
+    raised[...] = work[...]
+    stats[...] = rows[...]
+
+
+def probs_kernel(group, bias, q, g, ki, stats, raised, outer_stats, probs, rows_out, outer, inner, work, rows):
+    span = q.shape[0]
+
+    def finish(h, cols, products):
+        scores = products * (SCALE * LOG2E) + jnp.concatenate([bias[span : 2 * span]] * 2, axis=1)
+        own_peak, outer_peak = stats[h, 0:1, cols], outer_stats[h, 0:1, cols]
+        peak = jnp.maximum(jnp.maximum(own_peak, outer_peak), jnp.max(scores, axis=0, keepdims=True))
+        weight = jnp.exp2(scores - peak)
+        lowered, far = jnp.exp2(own_peak - peak), jnp.exp2(outer_peak - peak)
+        total = jnp.sum(weight, axis=0, keepdims=True) + lowered * stats[h, 1:2, cols]
+        scale = 1.0 / (total + far * outer_stats[h, 1:2, cols])
+        work[h, :span, cols] = (weight * scale).astype(jnp.bfloat16)
+        work[h, span:, cols] = (raised[h, :, cols].astype(jnp.float32) * (far * scale)).astype(jnp.bfloat16)
         rows[h, 0:1, cols] = lowered * scale
         rows[h, 1:2, cols] = lowered * scale * stats[h, 2:3, cols]
-        if first == (h + 1) * group - 2:
-            outs.append(dot(work[h], stack_heads(g, h * group, group), NN))
+
+    outs = by_pairs(
+        group,
+        ki.shape[1] // HEAD_DIM,
+        lambda h, first, cols: dot(head(ki, h), stack_heads(q, first, 2), NT),
+        finish,
+        lambda h: dot(work[h], stack_heads(g, h * group, group), NN),
+    )
     write_terms(outs, outer, inner)
     probs[...] = work[...]
-
-
-def scores_kernel(group, q, g, vi, vo, probs, rows, dscores, deltas, outer, inner, work):
-    outs = []
-    for h, first, cols in pairs(group, vi.shape[1] // HEAD_DIM):
-        if first == h * group:
-            values = stack_sources((vi, vo), h)
-        grad_probs = dot(values, stack_heads(g, first, 2), NT)
+    rows_out[...] = rows[...]
+
+
+def scores_kernel(group, q, g, vi, vo, probs, rows, dscores, deltas_out, outer, inner, work, deltas):
+    values = [stack_sources((vi, vo), h) for h in range(vi.shape[1] // HEAD_DIM)]
+
+    def finish(h, cols, grad_probs):
         weight = probs[h, :, cols].astype(jnp.float32)
         delta = rows[h, 1:2, cols] + jnp.sum(weight * grad_probs, axis=0, keepdims=True)
         work[h, :, cols] = (weight * (grad_probs - delta)).astype(jnp.bfloat16)
         deltas[h, 0:1, cols] = delta
-        if first == (h + 1) * group - 2:
-            outs.append(dot(work[h], stack_heads(q, h * group, group), NN) * SCALE)
+
+    outs = by_pairs(
+        group,
+        len(values),
+        lambda h, first, cols: dot(values[h], stack_heads(g, first, 2), NT),
+        finish,
+        lambda h: dot(work[h], stack_heads(q, h * group, group), NN) * SCALE,
+    )
     write_terms(outs, outer, inner)
     dscores[...] = work[...]
+    deltas_out[...] = deltas[...]
 
 
 def queries_kernel(
-    group, q, g, ks, ki, ko, raised, grad_probs, rows, deltas, dscores, dvi, dvo, dq, dk, dv, own_probs, own_scores
+    group, q, g, ks, ki, ko, raised, grad_probs, rows, deltas, dscores, dq, dk, dv, own_probs, own_scores
 ):
     f32, bf16 = jnp.float32, jnp.bfloat16
     kv_heads = ks.shape[1] // HEAD_DIM
@@ -167,8 +218,7 @@
     outs = []
     for h in range(kv_heads):
         lanes = slice(h * HEAD_DIM, (h + 1) * HEAD_DIM)
-        terms = dvi[:, lanes].astype(f32) + dvo[:, lanes].astype(f32)
-        dv[:, lanes] = (dot(own_probs[h], stack_heads(g, h * group, group), NN) + terms).astype(bf16)
+        dv[:, lanes] = dot(own_probs[h], stack_heads(g, h * group, group), NN)
         dk[:, lanes] = dot(own_scores[h], stack_heads(q, h * group, group), NN) * SCALE
         wide = jnp.concatenate([own_scores[h], dscores[h]], axis=0)
         outs.append((dot(stack_sources((ks, ki, ko), h), wide, TN) * SCALE).astype(bf16))
@@ -178,12 +228,13 @@
             dq[:, lanes] = out[:, e * HEAD_DIM : (e + 1) * HEAD_DIM].T
 
 
-def gate_kernel(x, vi, vo, out):
-    out[...] = x[...]
-
-
 def add_kernel(a, b, c, out):
     out[...] = (a[...] + b[...].astype(jnp.float32) + c[...].astype(jnp.float32)).astype(out.dtype)
+
+
+def last_kernel(values, a, b, c, dv, dk):
+    add_kernel(a, b, c, dk)
+    dv[...] = values[...]
 
 
 def shards(queries, keys, values, grad_out, stretch_order, block_keep):
@@ -203,7 +254,7 @@
     stat = jax.ShapeDtypeStruct((kv_heads, 8, wide), f32)
     kv32 = jax.ShapeDtypeStruct((span, width), f32)
     kv16 = jax.ShapeDtypeStruct((span, width), bf16)
-    work = [pltpu.VMEM(away.shape, bf16)]
+    work = [pltpu.VMEM(away.shape, bf16), pltpu.VMEM(stat.shape, f32)]
 
     def call(kernel, ins, out_shape, scratch=()):
         return pl.pallas_call(
@@ -231,24 +282,27 @@
     v_out = ring(v, "outer", 1)
     v_in = ring(v, "inner", 1)
     raised, grad_probs, stats = run(own_kernel, (bias, q, g, k, v), [own16, own32, stat])
+    outer_raised, outer_stats = run(
+        outer_kernel, (bias, q, k_out), [own16, stat], [pltpu.VMEM(own16.shape, bf16), pltpu.VMEM(stat.shape, f32)]
+    )
     probs, row_scale, dvo, dvi = run(
-        probs_kernel, (bias, q, g, k_in, k_out, stats), [away, stat, kv16, kv16], work
+        probs_kernel, (bias, q, g, k_in, stats, outer_raised, outer_stats), [away, stat, kv16, kv16], work
     )
     dv_in = ring(dvi, "inner", -1)
-    (dvo,) = call(gate_kernel, [vmem] * 3, [kv16])(dvo, v_in, v_out)
     dv_out = ring(dvo, "outer", -1)
     dscores, deltas, dko, dki = run(
         scores_kernel, (q, g, v_in, v_out, probs, row_scale), [away, stat, kv16, kv16], work
     )
     dk_in = ring(dki, "inner", -1)
     dk_out = ring(dko, "outer", -1)
-    dq, dks, dv = run(
+    dq, dks, dvs = run(
         queries_kernel,
-        (q, g, k, k_in, k_out, raised, grad_probs, row_scale, deltas, dscores, dv_in, dv_out),
-        [rows, kv32, kv16],
+        (q, g, k, k_in, k_out, raised, grad_probs, row_scale, deltas, dscores),
+        [rows, kv32, kv32],
         [pltpu.VMEM(own16.shape, bf16)] * 2,
     )
-    (dk,) = call(add_kernel, [vmem] * 3, [kv16])(dks, dk_in, dk_out)
+    (dv,) = call(add_kernel, [vmem] * 3, [kv16])(dvs, dv_out, dv_in)
+    dv, dk = call(last_kernel, [vmem] * 4, [kv16, kv16])(dv, dks, dk_in, dk_out)
     return dq, dk, dv
 
 

time: 28.8 us -> 28 us (0.972)
  waiting for transfers between devices: 4.69 us -> 4.16 us
  starting transfers between devices: 13.1 us -> 12.8 us
    ppermute x8, waiting for transfers between devices: 4.69 us -> 4.16 us  [ring(): lax.ppermute(block, axis, [(i, (i + step) % size) for i in range(size)])]
    pallas_call x4 -> x5, Pallas kernels: 7.77 us -> 7.72 us  [run(): call(functools.partial(kernel, group), [vmem] * len(ins), out_shape, scra...]
  transfers between devices with their start and end apart: 8 -> 8, of which waited for: 3 -> 2; matrix products, arithmetic and copies ran while one was open for 0% -> 0% of each run, Pallas kernels for 33% -> 34%
where the time goes in v4:
time: 28 us; the launch traced here: 27.9 us
  starting transfers between devices  12.8 us (46%)
  Pallas kernels  10.3 us (37%)
  waiting for transfers between devices  4.16 us (15%)
  between operations  0.68 us (2%)
    ppermute x8, starting transfers between devices, ring(): lax.ppermute(block, axis, [(i, (i + step) % size) for i in range(size)])  12.8 us
    pallas_call x5, Pallas kernels, run(): call(functools.partial(kernel, group), [vmem] * len(ins), out_shape, scra...  7.72 us
    ppermute x8, waiting for transfers between devices, ring(): lax.ppermute(block, axis, [(i, (i + step) % size) for i in range(size)])  4.16 us
    pallas_call x1, Pallas kernels, shards(): call(stage_kernel, [hbm] * 6, [rows, rows, kv16, kv16, jax.ShapeDtypeStru...  1.76 us
    pallas_call x1, Pallas kernels, shards(): dv, dk = call(last_kernel, [vmem] * 4, [kv16, kv16])(dv, dks, dk_in, dk_out)  0.73 us
  transfers between devices with their start and end apart: 8, of which 2 were waited for; matrix products, arithmetic and copies ran while one was open for 0% of the time, Pallas kernels for 34%

profile of v4, /device:TPU:1, one launch (start us, length us, event | category | flops | bytes accessed | tf_op | source)
XLA Modules:
  0.0 27.9 jit_solution(5520516197516306485)
XLA Ops:
  0.6 2.1 %collective-permute-start.1 = (bf16[128,512]{1,0:T(8,128)(2,1)}, bf16[128,512]{1,0:T(8,128)(2,1)S(1)}, u32[]{:S(2)}, u32[]{:S(2)}) collective-permute-start(bf16[128,512]{1,0:T(8,128)(2,1)} %keys.1), channel_id=1, source_target_pairs={{0,4},{4,8},{8,12},{12,16},{16,20},{20,24},{24,28},{28,32},{32,36}... | collective-permute-start | bytes 393224 | tf_op jit(solution)/shard_map/ppermute | solution.py:26
  2.8 3.8 %collective-permute-start = (bf16[128,512]{1,0:T(8,128)(2,1)}, bf16[128,512]{1,0:T(8,128)(2,1)S(1)}, u32[]{:S(2)}, u32[]{:S(2)}) collective-permute-start(bf16[128,512]{1,0:T(8,128)(2,1)} %keys.1), channel_id=1, source_target_pairs={{0,1},{1,2},{2,3},{3,0},{4,5},{5,6},{6,7},{7,4},{8,9},{9,10},{10,1... | collective-permute-start | bytes 393224 | tf_op jit(solution)/shard_map/ppermute | solution.py:26
  6.5 1.8 %shard_map.85 = (bf16[128,4096]{1,0:T(8,128)(2,1)S(1)}, bf16[128,4096]{1,0:T(8,128)(2,1)S(1)}, bf16[128,512]{1,0:T(8,128)(2,1)S(1)}, bf16[128,512]{1,0:T(8,128)(2,1)S(1)}, f32[384,128]{1,0:T(8,128)S(1)}) custom-call(s32[2,256]{1,0:T(2,128)} %bitcast.3, s32[3,2,2,256]{3,2,1,0:T(2,128)} %bitcast.2, bf16[128,4096]{1,0:T(8,128)(2,1)} %queries.1, ...), custom_call_target="tpu_custom_call" | custom-call | flops 1 | bytes 1 | tf_op jit(solution)/shard_map/pallas_call | solution.py:276
  8.3 1.3 %collective-permute-start.3 = (bf16[128,512]{1,0:T(8,128)(2,1)S(1)}, bf16[128,512]{1,0:T(8,128)(2,1)S(1)}, u32[]{:S(2)}, u32[]{:S(2)}) collective-permute-start(bf16[128,512]{1,0:T(8,128)(2,1)S(1)} %get-tuple-element.30.v), channel_id=1, source_target_pairs={{0,4},{4,8},{8,12},{12,16},{16,20},{20,24},{24,28},{28,32},{32,36}... | collective-permute-start | bytes 393224 | tf_op jit(solution)/shard_map/ppermute | solution.py:26
  9.6 0.3 %collective-permute-start.2 = (bf16[128,512]{1,0:T(8,128)(2,1)S(1)}, bf16[128,512]{1,0:T(8,128)(2,1)S(1)}, u32[]{:S(2)}, u32[]{:S(2)}) collective-permute-start(bf16[128,512]{1,0:T(8,128)(2,1)S(1)} %get-tuple-element.30.v), channel_id=1, source_target_pairs={{0,1},{1,2},{2,3},{3,0},{4,5},{5,6},{6,7},{7,4},{8,9},{9,10},{10,1... | collective-permute-start | bytes 393224 | tf_op jit(solution)/shard_map/ppermute | solution.py:26
  9.8 1.0 %shard_map.86 = (bf16[4,128,1024]{2,1,0:T(8,128)(2,1)S(1)}, f32[4,128,1024]{2,1,0:T(8,128)S(1)}, f32[4,8,1024]{2,1,0:T(8,128)S(1)}) custom-call(f32[384,128]{1,0:T(8,128)S(1)} %get-tuple-element.29.bias, bf16[128,4096]{1,0:T(8,128)(2,1)S(1)} %get-tuple-element.26.q, bf16[128,4096]{1,0:T(8,128)(2,1)S(1)} %get-tuple-element.27.g, ...), custom_call_target="tpu_custom_call" | custom-call | flops 1 | bytes 1 | tf_op jit(solution)/shard_map/pallas_call | solution.py:271
  10.9 2.9 %collective-permute-done.1.ko = bf16[128,512]{1,0:T(8,128)(2,1)S(1)} collective-permute-done((bf16[128,512]{1,0:T(8,128)(2,1)}, bf16[128,512]{1,0:T(8,128)(2,1)S(1)}, u32[]{:S(2)}, u32[]{:S(2)}) %collective-permute-start.1) | collective-permute-done | bytes 131104 | tf_op jit(solution)/shard_map/ppermute | solution.py:26
  13.8 0.9 %shard_map.87 = (bf16[4,128,1024]{2,1,0:T(8,128)(2,1)S(1)}, f32[4,8,1024]{2,1,0:T(8,128)S(1)}) custom-call(f32[384,128]{1,0:T(8,128)S(1)} %get-tuple-element.29.bias, bf16[128,4096]{1,0:T(8,128)(2,1)S(1)} %get-tuple-element.26.q, bf16[128,512]{1,0:T(8,128)(2,1)S(1)} %collective-permute-done.1.ko), custom_call_target="tpu_custom_call" | custom-call | flops 1 | bytes 1 | tf_op jit(solution)/shard_map/pallas_call | solution.py:271
  14.6 0.0 collective-permute-done.ki
  14.6 1.6 %shard_map.88 = (bf16[4,256,1024]{2,1,0:T(8,128)(2,1)S(1)}, f32[4,8,1024]{2,1,0:T(8,128)S(1)}, bf16[128,512]{1,0:T(8,128)(2,1)S(1)}, bf16[128,512]{1,0:T(8,128)(2,1)S(1)}) custom-call(f32[384,128]{1,0:T(8,128)S(1)} %get-tuple-element.29.bias, bf16[128,4096]{1,0:T(8,128)(2,1)S(1)} %get-tuple-element.26.q, bf16[128,4096]{1,0:T(8,128)(2,1)S(1)} %get-tuple-element.27.g, ...), custom_call_target="tpu_custom_call" | custom-call | flops 1 | bytes 1 | tf_op jit(solution)/shard_map/pallas_call | solution.py:271
  16.2 2.3 %collective-permute-start.4 = (bf16[128,512]{1,0:T(8,128)(2,1)S(1)}, bf16[128,512]{1,0:T(8,128)(2,1)S(1)}, u32[]{:S(2)}, u32[]{:S(2)}) collective-permute-start(bf16[128,512]{1,0:T(8,128)(2,1)S(1)} %get-tuple-element.42), channel_id=1, source_target_pairs={{0,252},{4,0},{8,4},{12,8},{16,12},{20,16},{24,20},{28,24},{32,28}... | collective-permute-start | bytes 393224 | tf_op jit(solution)/shard_map/ppermute | solution.py:26
  18.5 0.8 %collective-permute-start.5 = (bf16[128,512]{1,0:T(8,128)(2,1)S(1)}, bf16[128,512]{1,0:T(8,128)(2,1)S(1)}, u32[]{:S(2)}, u32[]{:S(2)}) collective-permute-start(bf16[128,512]{1,0:T(8,128)(2,1)S(1)} %get-tuple-element.43), channel_id=1, source_target_pairs={{0,3},{1,0},{2,1},{3,2},{4,7},{5,4},{6,5},{7,6},{8,11},{9,8},{10,9... | collective-permute-start | bytes 393224 | tf_op jit(solution)/shard_map/ppermute | solution.py:26
  19.3 0.0 collective-permute-done.3.vo
  19.3 0.0 collective-permute-done.2.vi
  19.3 1.9 %shard_map.89 = (bf16[4,256,1024]{2,1,0:T(8,128)(2,1)S(1)}, f32[4,8,1024]{2,1,0:T(8,128)S(1)}, bf16[128,512]{1,0:T(8,128)(2,1)S(1)}, bf16[128,512]{1,0:T(8,128)(2,1)S(1)}) custom-call(bf16[128,4096]{1,0:T(8,128)(2,1)S(1)} %get-tuple-element.26.q, bf16[128,4096]{1,0:T(8,128)(2,1)S(1)} %get-tuple-element.27.g, bf16[128,512]{1,0:T(8,128)(2,1)S(1)} %collective-permute-done.2.vi, ...), custom_call_target="tpu_custom_call" | custom-call | flops 1 | bytes 1 | tf_op jit(solution)/shard_map/pallas_call | solution.py:271
  21.2 1.3 %collective-permute-start.6 = (bf16[128,512]{1,0:T(8,128)(2,1)S(1)}, bf16[128,512]{1,0:T(8,128)(2,1)S(1)}, u32[]{:S(2)}, u32[]{:S(2)}) collective-permute-start(bf16[128,512]{1,0:T(8,128)(2,1)S(1)} %get-tuple-element.45), channel_id=1, source_target_pairs={{0,3},{1,0},{2,1},{3,2},{4,7},{5,4},{6,5},{7,6},{8,11},{9,8},{10,9... | collective-permute-start | bytes 393224 | tf_op jit(solution)/shard_map/ppermute | solution.py:26
  22.5 1.0 %collective-permute-start.7 = (bf16[128,512]{1,0:T(8,128)(2,1)S(1)}, bf16[128,512]{1,0:T(8,128)(2,1)S(1)}, u32[]{:S(2)}, u32[]{:S(2)}) collective-permute-start(bf16[128,512]{1,0:T(8,128)(2,1)S(1)} %get-tuple-element.46), channel_id=1, source_target_pairs={{0,252},{4,0},{8,4},{12,8},{16,12},{20,16},{24,20},{28,24},{32,28}... | collective-permute-start | bytes 393224 | tf_op jit(solution)/shard_map/ppermute | solution.py:26
  23.5 2.4 %shard_map.90 = (bf16[128,4096]{1,0:T(8,128)(2,1)}, f32[128,512]{1,0:T(8,128)S(1)}, f32[128,512]{1,0:T(8,128)S(1)}) custom-call(bf16[128,4096]{1,0:T(8,128)(2,1)S(1)} %get-tuple-element.26.q, bf16[128,4096]{1,0:T(8,128)(2,1)S(1)} %get-tuple-element.27.g, bf16[128,512]{1,0:T(8,128)(2,1)S(1)} %get-tuple-element.28.k.ks, ...), custom_call_target="tpu_custom_call" | custom-call | flops 1 | bytes 1 | tf_op jit(solution)/shard_map/pallas_call | solution.py:271
  25.9 0.0 collective-permute-done.4.b
  25.9 0.0 collective-permute-done.5.c
  25.9 1.2 %collective-permute-done.6.b = bf16[128,512]{1,0:T(8,128)(2,1)S(1)} collective-permute-done((bf16[128,512]{1,0:T(8,128)(2,1)S(1)}, bf16[128,512]{1,0:T(8,128)(2,1)S(1)}, u32[]{:S(2)}, u32[]{:S(2)}) %collective-permute-start.6) | collective-permute-done | bytes 131104 | tf_op jit(solution)/shard_map/ppermute | solution.py:26
  27.2 0.0 collective-permute-done.7.c
  27.2 0.7 %shard_map.92 = (bf16[128,512]{1,0:T(8,128)(2,1)}, bf16[128,512]{1,0:T(8,128)(2,1)}) custom-call(bf16[128,512]{1,0:T(8,128)(2,1)S(1)} %shard_map.91.values, f32[128,512]{1,0:T(8,128)S(1)} %get-tuple-element.44.a, bf16[128,512]{1,0:T(8,128)(2,1)S(1)} %collective-permute-done.6.b, bf16[128,512]{1,0:T(8,128)(2,1)S(1)} %collective-permute-done.7.c), custom_call_target="tpu_custom_call" | custom-call | flops 1 | bytes 1 | tf_op jit(solution)/shard_map/pallas_call | solution.py:305
  (1 shorter events, 0.0 us)
Async XLA Ops:
  0.6 13.1 %collective-permute-start.1 = (bf16[128,512]{1,0:T(8,128)(2,1)}, bf16[128,512]{1,0:T(8,128)(2,1)S(1)}, u32[]{:S(2)}, u32[]{:S(2)}) collective-permute-start(bf16[128,512]{1,0:T(8,128)(2,1)} %keys.1), channel_id=1, source_target_pairs={{0,4},{4,8},{8,12},{12,16},{16,20},{20,24},{24,28},{28,32},{32,36}... | collective-permute-start | bytes 393224 | tf_op jit(solution)/shard_map/ppermute | solution.py:26
  2.8 11.9 %collective-permute-start = (bf16[128,512]{1,0:T(8,128)(2,1)}, bf16[128,512]{1,0:T(8,128)(2,1)S(1)}, u32[]{:S(2)}, u32[]{:S(2)}) collective-permute-start(bf16[128,512]{1,0:T(8,128)(2,1)} %keys.1), channel_id=1, source_target_pairs={{0,1},{1,2},{2,3},{3,0},{4,5},{5,6},{6,7},{7,4},{8,9},{9,10},{10,1... | collective-permute-start | bytes 393224 | tf_op jit(solution)/shard_map/ppermute | solution.py:26
  8.3 11.0 %collective-permute-start.3 = (bf16[128,512]{1,0:T(8,128)(2,1)S(1)}, bf16[128,512]{1,0:T(8,128)(2,1)S(1)}, u32[]{:S(2)}, u32[]{:S(2)}) collective-permute-start(bf16[128,512]{1,0:T(8,128)(2,1)S(1)} %get-tuple-element.30.v), channel_id=1, source_target_pairs={{0,4},{4,8},{8,12},{12,16},{16,20},{20,24},{24,28},{28,32},{32,36}... | collective-permute-start | bytes 393224 | tf_op jit(solution)/shard_map/ppermute | solution.py:26
  9.6 9.7 %collective-permute-start.2 = (bf16[128,512]{1,0:T(8,128)(2,1)S(1)}, bf16[128,512]{1,0:T(8,128)(2,1)S(1)}, u32[]{:S(2)}, u32[]{:S(2)}) collective-permute-start(bf16[128,512]{1,0:T(8,128)(2,1)S(1)} %get-tuple-element.30.v), channel_id=1, source_target_pairs={{0,1},{1,2},{2,3},{3,0},{4,5},{5,6},{6,7},{7,4},{8,9},{9,10},{10,1... | collective-permute-start | bytes 393224 | tf_op jit(solution)/shard_map/ppermute | solution.py:26
  16.2 9.6 %collective-permute-start.4 = (bf16[128,512]{1,0:T(8,128)(2,1)S(1)}, bf16[128,512]{1,0:T(8,128)(2,1)S(1)}, u32[]{:S(2)}, u32[]{:S(2)}) collective-permute-start(bf16[128,512]{1,0:T(8,128)(2,1)S(1)} %get-tuple-element.42), channel_id=1, source_target_pairs={{0,252},{4,0},{8,4},{12,8},{16,12},{20,16},{24,20},{28,24},{32,28}... | collective-permute-start | bytes 393224 | tf_op jit(solution)/shard_map/ppermute | solution.py:26
  18.5 7.4 %collective-permute-start.5 = (bf16[128,512]{1,0:T(8,128)(2,1)S(1)}, bf16[128,512]{1,0:T(8,128)(2,1)S(1)}, u32[]{:S(2)}, u32[]{:S(2)}) collective-permute-start(bf16[128,512]{1,0:T(8,128)(2,1)S(1)} %get-tuple-element.43), channel_id=1, source_target_pairs={{0,3},{1,0},{2,1},{3,2},{4,7},{5,4},{6,5},{7,6},{8,11},{9,8},{10,9... | collective-permute-start | bytes 393224 | tf_op jit(solution)/shard_map/ppermute | solution.py:26
  21.2 6.0 %collective-permute-start.6 = (bf16[128,512]{1,0:T(8,128)(2,1)S(1)}, bf16[128,512]{1,0:T(8,128)(2,1)S(1)}, u32[]{:S(2)}, u32[]{:S(2)}) collective-permute-start(bf16[128,512]{1,0:T(8,128)(2,1)S(1)} %get-tuple-element.45), channel_id=1, source_target_pairs={{0,3},{1,0},{2,1},{3,2},{4,7},{5,4},{6,5},{7,6},{8,11},{9,8},{10,9... | collective-permute-start | bytes 393224 | tf_op jit(solution)/shard_map/ppermute | solution.py:26
  22.5 4.7 %collective-permute-start.7 = (bf16[128,512]{1,0:T(8,128)(2,1)S(1)}, bf16[128,512]{1,0:T(8,128)(2,1)S(1)}, u32[]{:S(2)}, u32[]{:S(2)}) collective-permute-start(bf16[128,512]{1,0:T(8,128)(2,1)S(1)} %get-tuple-element.46), channel_id=1, source_target_pairs={{0,252},{4,0},{8,4},{12,8},{16,12},{20,16},{24,20},{28,24},{32,28}... | collective-permute-start | bytes 393224 | tf_op jit(solution)/shard_map/ppermute | solution.py:26
